TPU v7x, 128 devices: a whole 4x4x4 slice. The times are simulated.
128 devices in a mesh: slab: 32 (over z, x, core), depth: 4 (over y).
Axes of the slice: x: 4, y: 4, z: 4, core: 2. Of those that a mesh axis runs over, the one named last changes fastest.
Arguments:
- alpha: float32 [512, 256, 512], P('slab', 'depth'), may hold values from 0 to 1
- vel_x: float32 [512, 256, 512], P('slab', 'depth'), may hold values from -1 to 1
- vel_z: float32 [512, 256, 512], P('slab', 'depth'), may hold values from -1 to 1
- divergence: float32 [512, 256, 512], P('slab', 'depth'), may hold values from -6 to 6
- press_guess: float32 [512, 256, 512], P('slab', 'depth'), may hold values from -6 to 6
- panel_records: bfloat16 [32768, 128], P(('slab', 'depth')), may hold values from -6 to 6
- panel_dest: int32 [32768, 1], P(('slab', 'depth')), may hold values from 0 to 127; in each aligned block of 256 rows (0 to 255, 256 to 511, ...) at most 4 rows name the same one
- panel_segment: int32 [32768, 1], P(('slab', 'depth')), may hold values from 0 to 4095
Outputs:
- pressure: float32 [512, 256, 512], P('slab', 'depth')
- alpha_next: float32 [512, 256, 512], P('slab', 'depth')
- panel_pressure: bfloat16 [32768, 128], P(('slab', 'depth'))
Inputs may be any that keep to these rules, and one draw needn't show every extreme that they name: `panel_dest`: among the 256 panels of one device no fluid device is named more than 4 times.
All inputs are finite; a program needn't handle non-finite values.
Results may differ from a plain program's by a relative error of at most 0.001.
Values may be sent and summed in bfloat16 or wider, within the bound.
A program may use at most 64 MiB of HBM per device.

v0:
```python
import jax
import jax.numpy as jnp
from jax import lax
from jax.sharding import PartitionSpec as P

COURANT = 0.2


def with_halo(block, sides, width):
    for axis, dim in sides:
        count = lax.axis_size(axis)
        forward = [(i, i + 1) for i in range(count - 1)]
        backward = [(target, source) for source, target in forward]
        low = lax.ppermute(
            lax.slice_in_dim(block, block.shape[dim] - width, None, axis=dim), axis, forward
        )
        high = lax.ppermute(lax.slice_in_dim(block, 0, width, axis=dim), axis, backward)
        block = jnp.concatenate([low, block, high], axis=dim)
    return block


def advect_core(alpha_pad, velx_pad, velz_pad):
    face_x = velx_pad[1:, 1:-1] * jnp.where(
        velx_pad[1:, 1:-1] > 0, alpha_pad[:-1, 1:-1], alpha_pad[1:, 1:-1]
    )
    face_z = velz_pad[1:-1, 1:] * jnp.where(
        velz_pad[1:-1, 1:] > 0, alpha_pad[1:-1, :-1], alpha_pad[1:-1, 1:]
    )
    change = face_x[1:] - face_x[:-1] + face_z[:, 1:] - face_z[:, :-1]
    return alpha_pad[1:-1, 1:-1] - COURANT * change


def sweep(press_pad, dens_pad, rhs):
    press_pad = jnp.pad(press_pad, ((0, 0), (0, 0), (1, 1)))
    dens_pad = jnp.pad(dens_pad, ((0, 0), (0, 0), (1, 1)))
    rows_all = rhs.shape[0]
    cols_all = rhs.shape[1]
    beam = rhs.shape[2]
    own_rho = dens_pad[1 : 1 + rows_all, 1 : 1 + cols_all, 1 : 1 + beam]
    total = jnp.zeros_like(rhs)
    weight = jnp.zeros_like(rhs)
    for off_x, off_z, off_y in ((0, 1, 1), (2, 1, 1), (1, 0, 1), (1, 2, 1), (1, 1, 0), (1, 1, 2)):
        next_p = press_pad[off_x : off_x + rows_all, off_z : off_z + cols_all, off_y : off_y + beam]
        next_rho = dens_pad[
            off_x : off_x + rows_all, off_z : off_z + cols_all, off_y : off_y + beam
        ]
        coeff = 2.0 / (own_rho + next_rho)
        total = total + coeff * next_p
        weight = weight + coeff
    return (total - rhs) / weight


def body(alpha, vel_x, vel_z, divergence, press_guess, panel_records, panel_dest, panel_segment):
    slabs = lax.axis_size("slab")
    depths = lax.axis_size("depth")
    devices = slabs * depths
    panel_count = panel_records.shape[0]
    capacity = 2 * panel_count // devices
    cells_x, cells_z, beam = alpha.shape
    blocks = beam // 128
    target = panel_dest[:, 0]
    onehot = (target[:, None] == jnp.arange(devices, dtype=jnp.int32)[None, :]).astype(jnp.int32)
    before = jnp.cumsum(onehot, axis=0) - onehot
    slot = jnp.sum(before * onehot, axis=1)
    place = target * capacity + slot
    send_rec = jnp.zeros((devices * capacity, 128), jnp.bfloat16).at[place].set(panel_records)
    send_seg = jnp.zeros((devices * capacity,), jnp.int32).at[place].set(panel_segment[:, 0])
    got_rec, got_seg = (
        lax.all_to_all(send_rec, ("slab", "depth"), split_axis=0, concat_axis=0, tiled=True),
        lax.all_to_all(send_seg, ("slab", "depth"), split_axis=0, concat_axis=0, tiled=True),
    )
    hull = (
        jnp.zeros((cells_x * cells_z * blocks, 128), jnp.float32)
        .at[got_seg]
        .add(got_rec.astype(jnp.float32))
    )
    hull = hull.reshape(cells_x, cells_z, beam)
    stacked = jnp.stack([alpha, vel_x, vel_z])
    padded = with_halo(stacked, (("slab", 1), ("depth", 2)), 1)
    alpha_next = advect_core(padded[0], padded[1], padded[2])
    density = 1.0 + 9.0 * alpha_next
    rhs = divergence + hull
    dens_pad = with_halo(density, (("slab", 0), ("depth", 1)), 1)
    pressure = press_guess
    for sweep_number in range(3):
        press_pad = with_halo(pressure, (("slab", 0), ("depth", 1)), 1)
        pressure = sweep(press_pad, dens_pad, rhs)
    wall_rows = pressure.reshape(-1, 128).astype(jnp.bfloat16)[got_seg]
    returned = lax.all_to_all(wall_rows, ("slab", "depth"), split_axis=0, concat_axis=0, tiled=True)
    panel_pressure = returned[place]
    return (pressure, alpha_next, panel_pressure)


def solution(mesh):
    in_specs = (
        P("slab", "depth", None),
        P("slab", "depth", None),
        P("slab", "depth", None),
        P("slab", "depth", None),
        P("slab", "depth", None),
        P(("slab", "depth"), None),
        P(("slab", "depth"), None),
        P(("slab", "depth"), None),
    )
    out_specs = (P("slab", "depth", None), P("slab", "depth", None), P(("slab", "depth"), None))
    return jax.shard_map(body, mesh=mesh, in_specs=in_specs, out_specs=out_specs, check_vma=False)
```

profile of v0, /device:TPU:1, one launch (start us, length us, event | category | flops | bytes accessed | tf_op | source)
XLA Modules:
  0.0 200.1 jit_solution(2018558820985501460)
XLA Ops:
  0.6 2.0 %pad_maximum_fusion.31 = (f32[3,1,64,512]{3,2,1,0:T(8,128)}, f32[3,1,64,512]{3,2,1,0:T(8,128)S(1)}) fusion(f32[1,16,64,512]{3,2,1,0:T(8,128)} %bitcast.35, f32[1,16,64,512]{3,2,1,0:T(8,128)} %bitcast.38, f32[1,16,64,512]{3,2,1,0:T(8,128)} %bitcast.41), kind=kLoop, calls=%fused_computation.120 | loop fusion | flops 393216 | bytes 7077888 | tf_op jit(solution)/shard_map/slice | solution.py:15
  2.7 4.5 %collective-permute-start = (f32[3,1,64,512]{3,2,1,0:T(8,128)}, f32[3,1,64,512]{3,2,1,0:T(8,128)S(1)}, u32[]{:S(2)}, u32[]{:S(2)}) collective-permute-start(f32[3,1,64,512]{3,2,1,0:T(8,128)} %get-tuple-element.14), channel_id=1, source_target_pairs={{0,4},{4,8},{8,12},{12,16},{16,20},{20,24},{24,28},{28,32},{32,36}... | collective-permute-start | bytes 1179656 | tf_op jit(solution)/shard_map/ppermute | solution.py:14
  7.2 1.9 collective-permute-start.1
  9.1 0.1 copy.14
  9.2 0.2 fusion.51
  9.5 0.2 fusion.53
  9.7 1.6 scatter_custom_fusion
  11.3 0.7 all_to_all.22
  12.0 10.6 %all-to-all-start = ((s32[128,4,1]{1,2,0:T(1,128)}), s32[128,4,1]{1,2,0:T(1,128)S(1)}, u32[]{:S(2)}, u32[]{:S(2)}) async-start(s32[128,4,1]{1,2,0:T(1,128)} %bitcast.14), calls=%async_computation | async-start | bytes 131072 | tf_op jit(solution)/shard_map/all_to_all | solution.py:70
  22.6 1.7 fusion.67
  24.3 3.5 %collective-permute-start.5 = (f32[1,64,512]{2,1,0:T(8,128)}, f32[1,64,512]{2,1,0:T(8,128)S(1)}, u32[]{:S(2)}, u32[]{:S(2)}) collective-permute-start(f32[1,64,512]{2,1,0:T(8,128)} %get-tuple-element.31), channel_id=1, source_target_pairs={{0,4},{4,8},{8,12},{12,16},{16,20},{20,24},{24,28},{28,32},{32,36}... | collective-permute-start | bytes 393224 | tf_op jit(solution)/shard_map/ppermute | solution.py:14
  27.9 1.9 collective-permute-start.7
  29.8 2.1 %scatter_custom_fusion.1 = bf16[512,128]{1,0:T(8,128)(2,1)} fusion(s32[256]{0:T(256)S(1)} %bitcast.55, bf16[256,128]{1,0:T(8,128)(2,1)} %param.13, bf16[]{:T(256)} %constant.8.clone.1), kind=kCustom, calls=%fused_computation.134 | custom fusion | bytes 131584 | tf_op jit(solution)/shard_map/scatter | solution.py:66
  31.9 0.3 all-to-all-done
  32.2 9.5 %all-to-all-start.1 = ((bf16[128,4,128]{2,1,0:T(4,128)(2,1)}), bf16[128,4,128]{2,1,0:T(4,128)(2,1)S(1)}, u32[]{:S(2)}, u32[]{:S(2)}) async-start(bf16[128,4,128]{2,1,0:T(4,128)(2,1)} %bitcast.16), calls=%async_computation.1 | async-start | bytes 262144 | tf_op jit(solution)/shard_map/all_to_all | solution.py:69
  41.8 0.5 broadcast.201
  42.3 0.8 reduce.3
  43.1 0.1 all_to_all.24
  43.2 8.4 %all-to-all-done.1 = bf16[128,4,128]{2,1,0:T(4,128)(2,1)S(1)} async-done(((bf16[128,4,128]{2,1,0:T(4,128)(2,1)}), bf16[128,4,128]{2,1,0:T(4,128)(2,1)S(1)}, u32[]{:S(2)}, u32[]{:S(2)}) %all-to-all-start.1) | async-done | bytes 131104 | tf_op jit(solution)/shard_map/all_to_all | solution.py:69
  51.6 3.8 %scatter_custom_fusion.2 = f32[4096,128]{1,0:T(8,128)} fusion(s32[512]{0:T(512)S(1)} %bitcast.51, f32[]{:T(128)} %constant.11.clone.1, bf16[512,128]{1,0:T(8,128)(2,1)S(1)} %bitcast.46), kind=kCustom, calls=%fused_computation.116 | custom fusion | flops 131072 | bytes 2228228 | tf_op jit(solution)/shard_map/scatter-add | solution.py:75
  55.4 2.9 %reshape.65 = f32[16,64,512]{2,1,0:T(8,128)} reshape(f32[4096,128]{1,0:T(8,128)} %scatter_custom_fusion.2) | data formatting | bytes 4194304 | tf_op jit(solution)/shard_map/reshape | solution.py:77
  58.3 2.0 %constant_dynamic-update-slice_fusion.1 = f32[18,64,512]{2,1,0:T(8,128)S(1)} fusion(f32[18,64,512]{2,1,0:T(8,128)S(1)} %constant_dynamic-update-slice_fusion.2, f32[16,64,512]{2,1,0:T(8,128)} %param.12), kind=kLoop, calls=%fused_computation.149 | loop fusion | bytes 4194304
  60.4 0.2 copy-done.1
  60.5 0.6 copy-done.2
  61.1 0.2 pad_maximum_fusion.36
  61.3 3.2 %collective-permute-start.2 = (f32[3,18,1,512]{3,2,1,0:T(1,128)S(1)}, f32[3,18,1,512]{3,2,1,0:T(1,128)S(1)}, u32[]{:S(2)}, u32[]{:S(2)}) collective-permute-start(f32[3,18,1,512]{3,2,1,0:T(1,128)S(1)} %get-tuple-element.12), channel_id=1, source_target_pairs={{0,1},{1,2},{2,3},{4,5},{5,6},{6,7},{8,9},{9,10},{10,11},{12,13},{... | collective-permute-start | bytes 331784 | tf_op jit(solution)/shard_map/ppermute | solution.py:14
  64.5 1.3 collective-permute-start.3
  65.9 1.2 collective-permute-done.2
  67.1 4.0 %collective-permute-done.3 = f32[3,18,1,512]{3,2,1,0:T(1,128)S(1)} collective-permute-done((f32[3,18,1,512]{3,2,1,0:T(1,128)S(1)}, f32[3,18,1,512]{3,2,1,0:T(1,128)S(1)}, u32[]{:S(2)}, u32[]{:S(2)}) %collective-permute-start.3) | collective-permute-done | bytes 110624 | tf_op jit(solution)/shard_map/ppermute | solution.py:17
  71.0 1.6 pad_maximum_fusion
  72.7 1.0 slice_bitcast_fusion.1
  73.6 0.7 fusion.2
  74.3 0.6 fusion.1
  74.9 0.9 multiply_add_fusion
  75.9 2.3 %collective-permute-start.4 = (f32[1,64,512]{2,1,0:T(8,128)S(1)}, f32[1,64,512]{2,1,0:T(8,128)S(1)}, u32[]{:S(2)}, u32[]{:S(2)}) collective-permute-start(f32[1,64,512]{2,1,0:T(8,128)S(1)} %get-tuple-element.29), channel_id=1, source_target_pairs={{0,4},{4,8},{8,12},{12,16},{16,20},{20,24},{24,28},{28,32},{32,36}... | collective-permute-start | bytes 393224 | tf_op jit(solution)/shard_map/ppermute | solution.py:14
  78.1 2.1 %collective-permute-start.6 = (f32[1,64,512]{2,1,0:T(8,128)S(1)}, f32[1,64,512]{2,1,0:T(8,128)S(1)}, u32[]{:S(2)}, u32[]{:S(2)}) collective-permute-start(f32[1,64,512]{2,1,0:T(8,128)S(1)} %get-tuple-element.28), channel_id=1, source_target_pairs={{4,0},{8,4},{12,8},{16,12},{20,16},{24,20},{28,24},{32,28},{36,32}... | collective-permute-start | bytes 393224 | tf_op jit(solution)/shard_map/ppermute | solution.py:17
  80.3 1.3 collective-permute-start.11
  81.6 4.0 %collective-permute-start.9 = (f32[18,1,512]{2,1,0:T(1,128)S(1)}, f32[18,1,512]{2,1,0:T(1,128)S(1)}, u32[]{:S(2)}, u32[]{:S(2)}) collective-permute-start(f32[18,1,512]{2,1,0:T(1,128)S(1)} %get-tuple-element.22), channel_id=1, source_target_pairs={{0,1},{1,2},{2,3},{4,5},{5,6},{6,7},{8,9},{9,10},{10,11},{12,13},{... | collective-permute-start | bytes 110600 | tf_op jit(solution)/shard_map/ppermute | solution.py:14
  85.6 1.3 collective-permute-start.10
  86.9 4.2 %collective-permute-start.8 = (f32[18,1,512]{2,1,0:T(1,128)S(1)}, f32[18,1,512]{2,1,0:T(1,128)S(1)}, u32[]{:S(2)}, u32[]{:S(2)}) collective-permute-start(f32[18,1,512]{2,1,0:T(1,128)S(1)} %get-tuple-element.21), channel_id=1, source_target_pairs={{0,1},{1,2},{2,3},{4,5},{5,6},{6,7},{8,9},{9,10},{10,11},{12,13},{... | collective-permute-start | bytes 110600 | tf_op jit(solution)/shard_map/ppermute | solution.py:14
  91.2 3.0 %select_maximum_fusion.8 = f32[18,66,514]{2,1,0:T(8,128)} fusion(f32[18,1,512]{2,1,0:T(1,128)S(1)} %collective-permute-done.11, f32[18,64,512]{2,1,0:T(8,128)S(1)} %constant_dynamic-update-slice_fusion, f32[18,1,512]{2,1,0:T(1,128)S(1)} %collective-permute-done.9), kind=kLoop, calls=%fused_computation.16 | loop fusion | flops 4885056 | bytes 4875552 | tf_op jit(solution)/shard_map/concatenate | solution.py:18
  94.2 3.0 %select_maximum_fusion.10 = f32[18,66,514]{2,1,0:T(8,128)S(1)} fusion(f32[18,1,512]{2,1,0:T(1,128)S(1)} %collective-permute-done.10, f32[18,1,512]{2,1,0:T(1,128)S(1)} %collective-permute-done.8, f32[1,64,512]{2,1,0:T(8,128)S(1)} %collective-permute-done.6, f32[16,64,512]{2,1,0:T(8,128)S(1)} %get-tuple-element.7, f32[1,64,512]{2,1,0:T(8,128)S(1)} %collective-permute-done.4), kind=kLoop, calls=%fused_computation.18 | loop fusion | flops 7327584 | bytes 4875552 | tf_op jit(solution)/shard_map/concatenate | solution.py:18
  97.2 12.9 %fusion.27 = (f32[16,64,512]{2,1,0:T(8,128)S(1)}, f32[16,64,512]{2,1,0:T(8,128)}) fusion(f32[18,66,514]{2,1,0:T(8,128)} %select_maximum_fusion.8, f32[18,1,512]{2,1,0:T(1,128)S(1)} %collective-permute-done.11, f32[18,64,512]{2,1,0:T(8,128)} %copy-done.6, f32[18,1,512]{2,1,0:T(1,128)S(1)} %collective-permute-done.9, ...), kind=kLoop, calls=%fused_computation.75 | loop fusion | flops 23592960 | bytes 26099712 | tf_op jit(solution)/shard_map/div | solution.py:50
  110.1 4.6 %collective-permute-start.12 = (f32[1,64,512]{2,1,0:T(8,128)S(1)}, f32[1,64,512]{2,1,0:T(8,128)S(1)}, u32[]{:S(2)}, u32[]{:S(2)}) collective-permute-start(f32[1,64,512]{2,1,0:T(8,128)S(1)} %get-tuple-element.26), channel_id=1, source_target_pairs={{0,4},{4,8},{8,12},{12,16},{16,20},{20,24},{24,28},{28,32},{32,36}... | collective-permute-start | bytes 393224 | tf_op jit(solution)/shard_map/ppermute | solution.py:14
  114.7 1.9 collective-permute-start.13
  116.7 4.3 %collective-permute-done.13 = f32[1,64,512]{2,1,0:T(8,128)S(1)} collective-permute-done((f32[1,64,512]{2,1,0:T(8,128)S(1)}, f32[1,64,512]{2,1,0:T(8,128)S(1)}, u32[]{:S(2)}, u32[]{:S(2)}) %collective-permute-start.13) | collective-permute-done | bytes 131104 | tf_op jit(solution)/shard_map/ppermute | solution.py:17
  121.1 2.3 %collective-permute-start.14 = (f32[18,1,512]{2,1,0:T(1,128)S(1)}, f32[18,1,512]{2,1,0:T(1,128)S(1)}, u32[]{:S(2)}, u32[]{:S(2)}) collective-permute-start(f32[18,1,512]{2,1,0:T(1,128)S(1)} %get-tuple-element.18), channel_id=1, source_target_pairs={{0,1},{1,2},{2,3},{4,5},{5,6},{6,7},{8,9},{9,10},{10,11},{12,13},{... | collective-permute-start | bytes 110600 | tf_op jit(solution)/shard_map/ppermute | solution.py:14
  123.4 1.4 collective-permute-start.15
  124.9 3.4 %collective-permute-done.15 = f32[18,1,512]{2,1,0:T(1,128)S(1)} collective-permute-done((f32[18,1,512]{2,1,0:T(1,128)S(1)}, f32[18,1,512]{2,1,0:T(1,128)S(1)}, u32[]{:S(2)}, u32[]{:S(2)}) %collective-permute-start.15) | collective-permute-done | bytes 36896 | tf_op jit(solution)/shard_map/ppermute | solution.py:17
  128.3 4.1 %select_maximum_fusion.4 = f32[18,66,514]{2,1,0:T(8,128)} fusion(f32[18,1,512]{2,1,0:T(1,128)S(1)} %collective-permute-done.15, f32[18,1,512]{2,1,0:T(1,128)S(1)} %collective-permute-done.14, f32[1,64,512]{2,1,0:T(8,128)S(1)} %collective-permute-done.13, f32[16,64,512]{2,1,0:T(8,128)S(1)} %get-tuple-element.5, f32[1,64,512]{2,1,0:T(8,128)S(1)} %collective-permute-done.12), kind=kLoop, calls=%fused_computation.12 | loop fusion | flops 7327584 | bytes 4875552 | tf_op jit(solution)/shard_map/concatenate | solution.py:18
  132.4 9.6 %fusion.16 = f32[16,64,512]{2,1,0:T(8,128)S(1)} fusion(f32[16,64,512]{2,1,0:T(8,128)S(1)} %copy-done.4, f32[18,66,514]{2,1,0:T(8,128)} %select_maximum_fusion.4, f32[18,1,512]{2,1,0:T(1,128)S(1)} %collective-permute-done.15, f32[1,64,512]{2,1,0:T(8,128)S(1)} %collective-permute-done.13, f32[16,64,512]{2,1,0:T(8,128)S(1)} %get-tuple-element.5, ...), kind=kLoop, calls=%fused_computation.54 | loop fusion | flops 25165824 | bytes 19546112 | tf_op jit(solution)/shard_map/div | solution.py:50
  142.1 3.3 %collective-permute-start.16 = (f32[1,64,512]{2,1,0:T(8,128)S(1)}, f32[1,64,512]{2,1,0:T(8,128)S(1)}, u32[]{:S(2)}, u32[]{:S(2)}) collective-permute-start(f32[1,64,512]{2,1,0:T(8,128)S(1)} %get-tuple-element.24), channel_id=1, source_target_pairs={{0,4},{4,8},{8,12},{12,16},{16,20},{20,24},{24,28},{28,32},{32,36}... | collective-permute-start | bytes 393224 | tf_op jit(solution)/shard_map/ppermute | solution.py:14
  145.4 1.9 collective-permute-start.17
  147.3 4.3 %collective-permute-done.17 = f32[1,64,512]{2,1,0:T(8,128)S(1)} collective-permute-done((f32[1,64,512]{2,1,0:T(8,128)S(1)}, f32[1,64,512]{2,1,0:T(8,128)S(1)}, u32[]{:S(2)}, u32[]{:S(2)}) %collective-permute-start.17) | collective-permute-done | bytes 131104 | tf_op jit(solution)/shard_map/ppermute | solution.py:17
  151.7 2.7 %collective-permute-start.18 = (f32[18,1,512]{2,1,0:T(1,128)S(1)}, f32[18,1,512]{2,1,0:T(1,128)S(1)}, u32[]{:S(2)}, u32[]{:S(2)}) collective-permute-start(f32[18,1,512]{2,1,0:T(1,128)S(1)} %get-tuple-element.16), channel_id=1, source_target_pairs={{0,1},{1,2},{2,3},{4,5},{5,6},{6,7},{8,9},{9,10},{10,11},{12,13},{... | collective-permute-start | bytes 110600 | tf_op jit(solution)/shard_map/ppermute | solution.py:14
  154.5 1.5 collective-permute-start.19
  156.0 3.1 %collective-permute-done.19 = f32[18,1,512]{2,1,0:T(1,128)S(1)} collective-permute-done((f32[18,1,512]{2,1,0:T(1,128)S(1)}, f32[18,1,512]{2,1,0:T(1,128)S(1)}, u32[]{:S(2)}, u32[]{:S(2)}) %collective-permute-start.19) | collective-permute-done | bytes 36896 | tf_op jit(solution)/shard_map/ppermute | solution.py:17
  159.2 4.1 %select_maximum_fusion = f32[18,66,514]{2,1,0:T(8,128)} fusion(f32[18,1,512]{2,1,0:T(1,128)S(1)} %collective-permute-done.19, f32[18,1,512]{2,1,0:T(1,128)S(1)} %collective-permute-done.18, f32[1,64,512]{2,1,0:T(8,128)S(1)} %collective-permute-done.17, f32[16,64,512]{2,1,0:T(8,128)S(1)} %fusion.16, f32[1,64,512]{2,1,0:T(8,128)S(1)} %collective-permute-done.16), kind=kLoop, calls=%fused_computation.8 | loop fusion | flops 7327584 | bytes 4875552 | tf_op jit(solution)/shard_map/concatenate | solution.py:18
  163.3 10.5 %fusion.60 = (bf16[16,64,512]{2,1,0:T(8,128)(2,1)S(1)}, f32[16,64,512]{2,1,0:T(8,128)}) fusion(f32[16,64,512]{2,1,0:T(8,128)S(1)} %copy-done.5, f32[18,66,514]{2,1,0:T(8,128)} %select_maximum_fusion, f32[18,66,514]{2,1,0:T(8,128)S(1)} %select_maximum_fusion.10, f32[16,64,512]{2,1,0:T(8,128)S(1)} %get-tuple-element.8, ...), kind=kLoop, calls=%fused_computation.157 | loop fusion | flops 25690112 | bytes 20594688 | tf_op jit(solution)/shard_map/convert_element_type | solution.py:88
  173.8 0.7 convert_element_type.31
  174.4 1.9 gather_fusion
  176.3 12.4 %all-to-all-start.2 = ((bf16[128,4,128]{2,1,0:T(4,128)(2,1)}), bf16[128,4,128]{2,1,0:T(4,128)(2,1)S(1)}, u32[]{:S(2)}, u32[]{:S(2)}) async-start(bf16[128,4,128]{2,1,0:T(4,128)(2,1)} %bitcast.18), calls=%async_computation.2 | async-start | bytes 262144 | tf_op jit(solution)/shard_map/all_to_all | solution.py:89
  188.8 9.8 %all-to-all-done.2 = bf16[128,4,128]{2,1,0:T(4,128)(2,1)S(1)} async-done(((bf16[128,4,128]{2,1,0:T(4,128)(2,1)}), bf16[128,4,128]{2,1,0:T(4,128)(2,1)S(1)}, u32[]{:S(2)}, u32[]{:S(2)}) %all-to-all-start.2) | async-done | bytes 131104 | tf_op jit(solution)/shard_map/all_to_all | solution.py:89
  198.6 1.5 gather_fusion.1
  (49 shorter events, 0.5 us)
Async XLA Ops:
  0.6 8.5 %copy-start.8 = (s32[256,1]{0,1:T(1,128)S(1)}, s32[256,1]{0,1:T(1,128)}, u32[]{:S(2)}) copy-start(s32[256,1]{0,1:T(1,128)} %param.14) | copy-start | bytes 3076
  2.7 57.7 %collective-permute-start = (f32[3,1,64,512]{3,2,1,0:T(8,128)}, f32[3,1,64,512]{3,2,1,0:T(8,128)S(1)}, u32[]{:S(2)}, u32[]{:S(2)}) collective-permute-start(f32[3,1,64,512]{3,2,1,0:T(8,128)} %get-tuple-element.14), channel_id=1, source_target_pairs={{0,4},{4,8},{8,12},{12,16},{16,20},{20,24},{24,28},{28,32},{32,36}... | collective-permute-start | bytes 1179656 | tf_op jit(solution)/shard_map/ppermute | solution.py:14
  7.2 53.2 %collective-permute-start.1 = (f32[3,1,64,512]{3,2,1,0:T(8,128)S(1)}, f32[3,1,64,512]{3,2,1,0:T(8,128)S(1)}, u32[]{:S(2)}, u32[]{:S(2)}) collective-permute-start(f32[3,1,64,512]{3,2,1,0:T(8,128)S(1)} %get-tuple-element.15), channel_id=1, source_target_pairs={{4,0},{8,4},{12,8},{16,12},{20,16},{24,20},{28,24},{32,28},{36,32}... | collective-permute-start | bytes 1179656 | tf_op jit(solution)/shard_map/ppermute | solution.py:17
  12.0 20.2 %all-to-all-start = ((s32[128,4,1]{1,2,0:T(1,128)}), s32[128,4,1]{1,2,0:T(1,128)S(1)}, u32[]{:S(2)}, u32[]{:S(2)}) async-start(s32[128,4,1]{1,2,0:T(1,128)} %bitcast.14), calls=%async_computation | async-start | bytes 131072 | tf_op jit(solution)/shard_map/all_to_all | solution.py:70
  24.3 33.9 %collective-permute-start.5 = (f32[1,64,512]{2,1,0:T(8,128)}, f32[1,64,512]{2,1,0:T(8,128)S(1)}, u32[]{:S(2)}, u32[]{:S(2)}) collective-permute-start(f32[1,64,512]{2,1,0:T(8,128)} %get-tuple-element.31), channel_id=1, source_target_pairs={{0,4},{4,8},{8,12},{12,16},{16,20},{20,24},{24,28},{28,32},{32,36}... | collective-permute-start | bytes 393224 | tf_op jit(solution)/shard_map/ppermute | solution.py:14
  27.9 38.0 %collective-permute-start.7 = (f32[1,64,512]{2,1,0:T(8,128)}, f32[1,64,512]{2,1,0:T(8,128)S(1)}, u32[]{:S(2)}, u32[]{:S(2)}) collective-permute-start(f32[1,64,512]{2,1,0:T(8,128)} %get-tuple-element.30), channel_id=1, source_target_pairs={{4,0},{8,4},{12,8},{16,12},{20,16},{24,20},{28,24},{32,28},{36,32}... | collective-permute-start | bytes 393224 | tf_op jit(solution)/shard_map/ppermute | solution.py:17
  32.2 19.4 %all-to-all-start.1 = ((bf16[128,4,128]{2,1,0:T(4,128)(2,1)}), bf16[128,4,128]{2,1,0:T(4,128)(2,1)S(1)}, u32[]{:S(2)}, u32[]{:S(2)}) async-start(bf16[128,4,128]{2,1,0:T(4,128)(2,1)} %bitcast.16), calls=%async_computation.1 | async-start | bytes 262144 | tf_op jit(solution)/shard_map/all_to_all | solution.py:69
  55.4 4.9 %copy-start.3 = (f32[16,64,512]{2,1,0:T(8,128)S(1)}, f32[16,64,512]{2,1,0:T(8,128)}, u32[]{:S(2)}) copy-start(f32[16,64,512]{2,1,0:T(8,128)} %param.8) | copy-start | bytes 6291460
  58.3 2.2 %copy-start.1 = (f32[16,64,512]{2,1,0:T(8,128)S(1)}, f32[16,64,512]{2,1,0:T(8,128)}, u32[]{:S(2)}) copy-start(f32[16,64,512]{2,1,0:T(8,128)} %param.10) | copy-start | bytes 6291460
  58.3 2.8 %copy-start.2 = (f32[16,64,512]{2,1,0:T(8,128)S(1)}, f32[16,64,512]{2,1,0:T(8,128)}, u32[]{:S(2)}) copy-start(f32[16,64,512]{2,1,0:T(8,128)} %param.9) | copy-start | bytes 6291460
  61.3 5.7 %collective-permute-start.2 = (f32[3,18,1,512]{3,2,1,0:T(1,128)S(1)}, f32[3,18,1,512]{3,2,1,0:T(1,128)S(1)}, u32[]{:S(2)}, u32[]{:S(2)}) collective-permute-start(f32[3,18,1,512]{3,2,1,0:T(1,128)S(1)} %get-tuple-element.12), channel_id=1, source_target_pairs={{0,1},{1,2},{2,3},{4,5},{5,6},{6,7},{8,9},{9,10},{10,11},{12,13},{... | collective-permute-start | bytes 331784 | tf_op jit(solution)/shard_map/ppermute | solution.py:14
  64.5 6.5 %collective-permute-start.3 = (f32[3,18,1,512]{3,2,1,0:T(1,128)S(1)}, f32[3,18,1,512]{3,2,1,0:T(1,128)S(1)}, u32[]{:S(2)}, u32[]{:S(2)}) collective-permute-start(f32[3,18,1,512]{3,2,1,0:T(1,128)S(1)} %get-tuple-element.13), channel_id=1, source_target_pairs={{1,0},{2,1},{3,2},{5,4},{6,5},{7,6},{9,8},{10,9},{11,10},{13,12},{... | collective-permute-start | bytes 331784 | tf_op jit(solution)/shard_map/ppermute | solution.py:17
  65.8 25.3 %copy-start.6 = (f32[18,64,512]{2,1,0:T(8,128)}, f32[18,64,512]{2,1,0:T(8,128)S(1)}, u32[]{:S(2)}) copy-start(f32[18,64,512]{2,1,0:T(8,128)S(1)} %constant_dynamic-update-slice_fusion) | copy-start | bytes 7077892
  75.8 87.5 %copy-start = (f32[16,64,512]{2,1,0:T(8,128)}, f32[16,64,512]{2,1,0:T(8,128)S(1)}, u32[]{:S(2)}) copy-start(f32[16,64,512]{2,1,0:T(8,128)S(1)} %get-tuple-element.8) | copy-start | bytes 6291460
  75.9 9.7 %collective-permute-start.4 = (f32[1,64,512]{2,1,0:T(8,128)S(1)}, f32[1,64,512]{2,1,0:T(8,128)S(1)}, u32[]{:S(2)}, u32[]{:S(2)}) collective-permute-start(f32[1,64,512]{2,1,0:T(8,128)S(1)} %get-tuple-element.29), channel_id=1, source_target_pairs={{0,4},{4,8},{8,12},{12,16},{16,20},{20,24},{24,28},{28,32},{32,36}... | collective-permute-start | bytes 393224 | tf_op jit(solution)/shard_map/ppermute | solution.py:14
  78.1 7.5 %collective-permute-start.6 = (f32[1,64,512]{2,1,0:T(8,128)S(1)}, f32[1,64,512]{2,1,0:T(8,128)S(1)}, u32[]{:S(2)}, u32[]{:S(2)}) collective-permute-start(f32[1,64,512]{2,1,0:T(8,128)S(1)} %get-tuple-element.28), channel_id=1, source_target_pairs={{4,0},{8,4},{12,8},{16,12},{20,16},{24,20},{28,24},{32,28},{36,32}... | collective-permute-start | bytes 393224 | tf_op jit(solution)/shard_map/ppermute | solution.py:17
  80.3 10.9 %collective-permute-start.11 = (f32[18,1,512]{2,1,0:T(1,128)S(1)}, f32[18,1,512]{2,1,0:T(1,128)S(1)}, u32[]{:S(2)}, u32[]{:S(2)}) collective-permute-start(f32[18,1,512]{2,1,0:T(1,128)S(1)} %get-tuple-element.23), channel_id=1, source_target_pairs={{1,0},{2,1},{3,2},{5,4},{6,5},{7,6},{9,8},{10,9},{11,10},{13,12},{... | collective-permute-start | bytes 110600 | tf_op jit(solution)/shard_map/ppermute | solution.py:17
  81.6 9.6 %collective-permute-start.9 = (f32[18,1,512]{2,1,0:T(1,128)S(1)}, f32[18,1,512]{2,1,0:T(1,128)S(1)}, u32[]{:S(2)}, u32[]{:S(2)}) collective-permute-start(f32[18,1,512]{2,1,0:T(1,128)S(1)} %get-tuple-element.22), channel_id=1, source_target_pairs={{0,1},{1,2},{2,3},{4,5},{5,6},{6,7},{8,9},{9,10},{10,11},{12,13},{... | collective-permute-start | bytes 110600 | tf_op jit(solution)/shard_map/ppermute | solution.py:14
  85.6 8.5 %collective-permute-start.10 = (f32[18,1,512]{2,1,0:T(1,128)S(1)}, f32[18,1,512]{2,1,0:T(1,128)S(1)}, u32[]{:S(2)}, u32[]{:S(2)}) collective-permute-start(f32[18,1,512]{2,1,0:T(1,128)S(1)} %get-tuple-element.20), channel_id=1, source_target_pairs={{1,0},{2,1},{3,2},{5,4},{6,5},{7,6},{9,8},{10,9},{11,10},{13,12},{... | collective-permute-start | bytes 110600 | tf_op jit(solution)/shard_map/ppermute | solution.py:17
  86.9 7.2 %collective-permute-start.8 = (f32[18,1,512]{2,1,0:T(1,128)S(1)}, f32[18,1,512]{2,1,0:T(1,128)S(1)}, u32[]{:S(2)}, u32[]{:S(2)}) collective-permute-start(f32[18,1,512]{2,1,0:T(1,128)S(1)} %get-tuple-element.21), channel_id=1, source_target_pairs={{0,1},{1,2},{2,3},{4,5},{5,6},{6,7},{8,9},{9,10},{10,11},{12,13},{... | collective-permute-start | bytes 110600 | tf_op jit(solution)/shard_map/ppermute | solution.py:14
  94.1 3.0 %copy-start.7 = (f32[16,64,512]{2,1,0:T(8,128)S(1)}, f32[16,64,512]{2,1,0:T(8,128)}, u32[]{:S(2)}) copy-start(f32[16,64,512]{2,1,0:T(8,128)} %param.12) | copy-start | bytes 6291460
  110.1 6.6 %collective-permute-start.12 = (f32[1,64,512]{2,1,0:T(8,128)S(1)}, f32[1,64,512]{2,1,0:T(8,128)S(1)}, u32[]{:S(2)}, u32[]{:S(2)}) collective-permute-start(f32[1,64,512]{2,1,0:T(8,128)S(1)} %get-tuple-element.26), channel_id=1, source_target_pairs={{0,4},{4,8},{8,12},{12,16},{16,20},{20,24},{24,28},{28,32},{32,36}... | collective-permute-start | bytes 393224 | tf_op jit(solution)/shard_map/ppermute | solution.py:14
  114.7 6.3 %collective-permute-start.13 = (f32[1,64,512]{2,1,0:T(8,128)S(1)}, f32[1,64,512]{2,1,0:T(8,128)S(1)}, u32[]{:S(2)}, u32[]{:S(2)}) collective-permute-start(f32[1,64,512]{2,1,0:T(8,128)S(1)} %get-tuple-element.27), channel_id=1, source_target_pairs={{4,0},{8,4},{12,8},{16,12},{20,16},{24,20},{28,24},{32,28},{36,32}... | collective-permute-start | bytes 393224 | tf_op jit(solution)/shard_map/ppermute | solution.py:17
  121.1 3.8 %collective-permute-start.14 = (f32[18,1,512]{2,1,0:T(1,128)S(1)}, f32[18,1,512]{2,1,0:T(1,128)S(1)}, u32[]{:S(2)}, u32[]{:S(2)}) collective-permute-start(f32[18,1,512]{2,1,0:T(1,128)S(1)} %get-tuple-element.18), channel_id=1, source_target_pairs={{0,1},{1,2},{2,3},{4,5},{5,6},{6,7},{8,9},{9,10},{10,11},{12,13},{... | collective-permute-start | bytes 110600 | tf_op jit(solution)/shard_map/ppermute | solution.py:14
  123.4 9.0 %copy-start.4 = (f32[16,64,512]{2,1,0:T(8,128)S(1)}, f32[16,64,512]{2,1,0:T(8,128)}, u32[]{:S(2)}) copy-start(f32[16,64,512]{2,1,0:T(8,128)} %get-tuple-element.6) | copy-start | bytes 6291460
  123.4 4.8 %collective-permute-start.15 = (f32[18,1,512]{2,1,0:T(1,128)S(1)}, f32[18,1,512]{2,1,0:T(1,128)S(1)}, u32[]{:S(2)}, u32[]{:S(2)}) collective-permute-start(f32[18,1,512]{2,1,0:T(1,128)S(1)} %get-tuple-element.19), channel_id=1, source_target_pairs={{1,0},{2,1},{3,2},{5,4},{6,5},{7,6},{9,8},{10,9},{11,10},{13,12},{... | collective-permute-start | bytes 110600 | tf_op jit(solution)/shard_map/ppermute | solution.py:17
  142.1 5.2 %collective-permute-start.16 = (f32[1,64,512]{2,1,0:T(8,128)S(1)}, f32[1,64,512]{2,1,0:T(8,128)S(1)}, u32[]{:S(2)}, u32[]{:S(2)}) collective-permute-start(f32[1,64,512]{2,1,0:T(8,128)S(1)} %get-tuple-element.24), channel_id=1, source_target_pairs={{0,4},{4,8},{8,12},{12,16},{16,20},{20,24},{24,28},{28,32},{32,36}... | collective-permute-start | bytes 393224 | tf_op jit(solution)/shard_map/ppermute | solution.py:14
  145.4 6.3 %collective-permute-start.17 = (f32[1,64,512]{2,1,0:T(8,128)S(1)}, f32[1,64,512]{2,1,0:T(8,128)S(1)}, u32[]{:S(2)}, u32[]{:S(2)}) collective-permute-start(f32[1,64,512]{2,1,0:T(8,128)S(1)} %get-tuple-element.25), channel_id=1, source_target_pairs={{4,0},{8,4},{12,8},{16,12},{20,16},{24,20},{28,24},{32,28},{36,32}... | collective-permute-start | bytes 393224 | tf_op jit(solution)/shard_map/ppermute | solution.py:17
  151.7 4.3 %collective-permute-start.18 = (f32[18,1,512]{2,1,0:T(1,128)S(1)}, f32[18,1,512]{2,1,0:T(1,128)S(1)}, u32[]{:S(2)}, u32[]{:S(2)}) collective-permute-start(f32[18,1,512]{2,1,0:T(1,128)S(1)} %get-tuple-element.16), channel_id=1, source_target_pairs={{0,1},{1,2},{2,3},{4,5},{5,6},{6,7},{8,9},{9,10},{10,11},{12,13},{... | collective-permute-start | bytes 110600 | tf_op jit(solution)/shard_map/ppermute | solution.py:14
  154.5 4.7 %collective-permute-start.19 = (f32[18,1,512]{2,1,0:T(1,128)S(1)}, f32[18,1,512]{2,1,0:T(1,128)S(1)}, u32[]{:S(2)}, u32[]{:S(2)}) collective-permute-start(f32[18,1,512]{2,1,0:T(1,128)S(1)} %get-tuple-element.17), channel_id=1, source_target_pairs={{1,0},{2,1},{3,2},{5,4},{6,5},{7,6},{9,8},{10,9},{11,10},{13,12},{... | collective-permute-start | bytes 110600 | tf_op jit(solution)/shard_map/ppermute | solution.py:17
  156.0 7.3 %copy-start.5 = (f32[16,64,512]{2,1,0:T(8,128)S(1)}, f32[16,64,512]{2,1,0:T(8,128)}, u32[]{:S(2)}) copy-start(f32[16,64,512]{2,1,0:T(8,128)} %get-tuple-element.6) | copy-start | bytes 6291460
  176.3 22.3 %all-to-all-start.2 = ((bf16[128,4,128]{2,1,0:T(4,128)(2,1)}), bf16[128,4,128]{2,1,0:T(4,128)(2,1)S(1)}, u32[]{:S(2)}, u32[]{:S(2)}) async-start(bf16[128,4,128]{2,1,0:T(4,128)(2,1)} %bitcast.18), calls=%async_computation.2 | async-start | bytes 262144 | tf_op jit(solution)/shard_map/all_to_all | solution.py:89
where the time goes:
time: 201 us; the launch traced here: 200 us
  starting transfers between devices  83.7 us (42%)
  other arithmetic  58.5 us (29%)
  waiting for transfers between devices  39 us (19%)
  local copies, waits for them, and re-layouts  17.7 us (9%)
    ppermute x10, starting transfers between devices, with_halo(): lax.ppermute(lax.slice_in_dim(block, block.shape[dim] - width, None, axis...  34.6 us
    div x2, other arithmetic, sweep(): return (total - rhs) / weight  22.6 us
    ppermute x10, waiting for transfers between devices, with_halo(): lax.ppermute(lax.slice_in_dim(block, 0, width, axis=dim), axis, backward)  19.2 us
    ppermute x10, starting transfers between devices, with_halo(): lax.ppermute(lax.slice_in_dim(block, 0, width, axis=dim), axis, backward)  16.6 us
    concatenate x6, other arithmetic, with_halo(): block = jnp.concatenate([low, block, high], axis=dim)  15.9 us
    all_to_all x1, starting transfers between devices, body(): lax.all_to_all(wall_rows, ('slab', 'depth'), split_axis=0, concat_axis=0,...  12.4 us
    all_to_all x1, starting transfers between devices, body(): lax.all_to_all(send_seg, ('slab', 'depth'), split_axis=0, concat_axis=0,...  10.6 us
    convert_element_type x1, other arithmetic, body(): wall_rows = pressure.reshape(-1, 128).astype(jnp.bfloat16)[got_seg]  10.5 us
  transfers between devices with their start and end apart: 23, of which 9 were waited for; matrix products, arithmetic and copies ran while one was open for 10% of the time, Pallas kernels for 0%

commit v1 on v0

v1 whole, which is shorter than its diff:
```python
import jax
import jax.numpy as jnp
from jax import lax
from jax.experimental import pallas as pl
from jax.experimental.pallas import tpu as pltpu
from jax.sharding import PartitionSpec as P

MESH = pl.DeviceIdType.MESH
F32, BF16, I32 = jnp.float32, jnp.bfloat16, jnp.int32
CX, CZ, BEAM, LANES = 16, 64, 512, 128
NB = BEAM // LANES
ROW0 = 8
PADZ = CZ + 16
SLABS, DEPTHS = 32, 4
GA, GB = 8, 16
CAP = 4
SLOTS = GA * GB * CAP
PAN = 256
REC_B, REC_A = GA * CAP, GB * CAP
META = 16


def iota(shape, dim):
    return lax.broadcasted_iota(I32, shape, dim)


def onehot(cond):
    return jnp.where(cond, 1.0, 0.0).astype(BF16)


def dot(a, b):
    return jnp.dot(a, b, preferred_element_type=F32)


def recip(d):
    r = pl.reciprocal(d, approx=True)
    return r * (2.0 - d * r)


def kernel(
    alpha_h, velx_h, velz_h, div_h, press_h, rec_ref, dest_ref, seg_ref,
    press_o, alpha_o, panel_o,
    al, vx, vz, div, rho, p0, p1, p2, an_s, pr_s,
    axm, axp, azm, azp, aym, ayp, rr,
    zs, zr,
    s1, r1, s2, r2, s3, t1, s4, t2,
    q_s, g_s, perm_s, rmat, pb,
    load_sem, out_sem, xs_sem, xr_sem, zs_sem, zr_sem,
    b1s, b1r, a1s, a1r, a2s, a2r, b2s, b2r,
):
    slab = lax.axis_index("slab")
    depth = lax.axis_index("depth")
    up_s, dn_s = (slab + 1) % SLABS, (slab + SLABS - 1) % SLABS
    up_d, dn_d = (depth + 1) % DEPTHS, (depth + DEPTHS - 1) % DEPTHS
    x_up, x_dn = (up_s, depth), (dn_s, depth)
    z_up, z_dn = (slab, up_d), (slab, dn_d)
    b_me, core = slab // 2, slab % 2
    a_me = core * DEPTHS + depth

    def b_peer(k):
        b = (b_me + k) % GB
        return b, (b * 2 + core, depth)

    def a_peer(k):
        a = (a_me + k) % GA
        return a, (b_me * 2 + a // DEPTHS, a % DEPTHS)

    loads = {}
    sem_i = 0
    for name, src, dst in (
        ("al", alpha_h, lambda y: al.at[pl.ds(1, CX), y, pl.ds(ROW0, CZ), :]),
        ("vx", velx_h, lambda y: vx.at[pl.ds(0, CX), y, :, :]),
        ("vz", velz_h, lambda y: vz.at[:, y, pl.ds(0, CZ), :]),
        ("p0", press_h, lambda y: p0.at[pl.ds(1, CX), y, pl.ds(ROW0, CZ), :]),
        ("div", div_h, lambda y: div.at[:, y, :, :]),
    ):
        loads[name] = []
        for y in range(NB):
            c = pltpu.make_async_copy(
                src.at[:, :, pl.ds(y * LANES, LANES)], dst(y), load_sem.at[sem_i]
            )
            c.start()
            sem_i += 1
            loads[name].append(c)

    barrier = pltpu.get_barrier_semaphore()
    for dev in (x_up, x_dn, z_up, z_dn):
        pl.semaphore_signal(barrier, inc=1, device_id=dev, device_id_type=MESH)

    def sig_b(k, c):
        pl.semaphore_signal(barrier, inc=1, device_id=b_peer(k)[1], device_id_type=MESH)
        return c

    def sig_a(k, c):
        pl.semaphore_signal(barrier, inc=1, device_id=a_peer(k)[1], device_id_type=MESH)
        return c

    lax.fori_loop(1, GB, sig_b, 0)
    lax.fori_loop(1, GA, sig_a, 0)

    dest, seg = dest_ref[...], seg_ref[...]
    own = onehot(iota((GA * GB, PAN), 0) == dest)
    before = dot(own, onehot(iota((PAN, PAN), 0) < iota((PAN, PAN), 1)))
    slot = jnp.sum(own.astype(F32) * before, axis=0, keepdims=True)
    place = dest * CAP + slot.astype(I32)
    packed = dot(onehot(iota((SLOTS, PAN), 0) == place), rec_ref[...]).astype(BF16)
    lane_of = place & (REC_B - 1)
    row = iota((LANES, PAN), 0)
    hi, lo = (seg >> 6).astype(F32), (seg & 63).astype(F32)
    bt = jnp.where(row == lane_of, hi, 0.0) + jnp.where(row == lane_of + REC_B, lo, 0.0)
    meta = lax.dot_general(
        onehot(iota((GB, PAN), 0) == (dest >> 3)), bt.astype(BF16),
        (((1,), (1,)), ((), ())), preferred_element_type=F32,
    )
    for b in range(GB):
        s1[b, 0:REC_B, :] = packed[b * REC_B : (b + 1) * REC_B]
        s1[b, REC_B:, :] = jnp.broadcast_to(meta[b : b + 1], (META, LANES)).astype(BF16)
    place_t = jnp.broadcast_to(place.astype(F32), (LANES, PAN)).T
    for c in range(SLOTS // LANES):
        q_s[:, c * LANES : (c + 1) * LANES] = onehot(
            place_t == (iota((PAN, LANES), 1) + c * LANES).astype(F32)
        )

    def rcopy(src, dst, ss, rs, dev):
        return pltpu.make_async_remote_copy(
            src_ref=src, dst_ref=dst, send_sem=ss, recv_sem=rs,
            device_id=dev, device_id_type=MESH,
        )

    def xcopy(i, src, src_x, dst_x, dev, padded=True):
        rows = pl.ds(ROW0, CZ) if padded else pl.ds(0, CZ)
        return rcopy(
            src.at[src_x, :, rows, :], src.at[dst_x, :, rows, :], xs_sem.at[i], xr_sem.at[i], dev
        )

    def zcopy(i, dev):
        return rcopy(zs.at[i], zr.at[i], zs_sem.at[i], zr_sem.at[i], dev)

    def xpair(i, ref):
        return [xcopy(i, ref, CX, 0, x_up), xcopy(i + 1, ref, 1, CX + 1, x_dn)]

    def zpair(i):
        return [zcopy(i, z_up), zcopy(i + 1, z_dn)]

    def pack_z(items):
        def step(x, c):
            for i, ref, xo, r in items:
                zs[i, x] = ref[x + xo, :, r, :]
            return c

        lax.fori_loop(0, CX, step, 0)

    def fill_z(items):
        def step(x, c):
            for i, ref, xo, r, edge in items:
                zero = depth == edge
                ref[x + xo, :, r, :] = jnp.where(zero, 0.0, zr[i, x])
            return c

        lax.fori_loop(0, CX, step, 0)

    def zero_x(ref):
        @pl.when(slab == 0)
        def _():
            ref[0, :, ROW0 : ROW0 + CZ, :] = jnp.zeros((NB, CZ, LANES), F32)

        @pl.when(slab == SLABS - 1)
        def _():
            ref[CX + 1, :, ROW0 : ROW0 + CZ, :] = jnp.zeros((NB, CZ, LANES), F32)

    sends = []

    def start(copies):
        for c in copies:
            c.start()
        sends.extend(copies)

    for name in ("al", "vx", "vz"):
        for c in loads[name]:
            c.wait()
    pack_z([(0, al, 1, ROW0 + CZ - 1), (1, al, 1, ROW0), (2, vz, 0, 0)])
    pl.semaphore_wait(barrier, 4 + (GB - 1) + (GA - 1))
    e_al, e_vx = xpair(0, al), [xcopy(2, vx, 0, CX, x_dn, padded=False)]
    ez_al, ez_vz = zpair(0), [zcopy(2, z_dn)]
    start(e_al + e_vx + ez_al + ez_vz)

    def b1_copy(k):
        b, dev = b_peer(k)
        return rcopy(s1.at[b], r1.at[b_me], b1s.at[k], b1r.at[k], dev)

    def b1_start(k, c):
        b1_copy(k).start()
        return c

    lax.fori_loop(1, GB, b1_start, 0)
    r1[b_me] = s1[b_me]

    for c in loads["p0"]:
        c.wait()
    pack_z([(3, p0, 1, ROW0 + CZ - 1), (4, p0, 1, ROW0)])
    e_p0, ez_p0 = xpair(3, p0), zpair(3)
    start(e_p0 + ez_p0)

    lane = iota((NB, 8, LANES), 2)
    zero1 = jnp.zeros((1, 8, LANES), F32)

    def y_minus(v):
        r = pltpu.roll(v, 1, 2)
        return jnp.where(lane == 0, jnp.concatenate([zero1, r[: NB - 1]], axis=0), r)

    def y_plus(v):
        r = pltpu.roll(v, LANES - 1, 2)
        return jnp.where(lane == LANES - 1, jnp.concatenate([r[1:], zero1], axis=0), r)

    def at(ref, x, z, shift=0):
        return ref[x, :, pl.ds(ROW0 + z * 8 + shift, 8), :]

    def raw(ref, x, z, shift=0):
        return ref[x, :, pl.ds(z * 8 + shift, 8), :]

    def to_out(ref, x, z, v):
        for y in range(NB):
            ref[x, pl.ds(z * 8, 8), y * LANES : (y + 1) * LANES] = v[y]

    def advect(x, z):
        a = at(al, x + 1, z)
        u0, u1 = raw(vx, x, z), raw(vx, x + 1, z)
        w0, w1 = raw(vz, x, z), raw(vz, x, z, 1)
        fx0 = u0 * jnp.where(u0 > 0, at(al, x, z), a)
        fx1 = u1 * jnp.where(u1 > 0, a, at(al, x + 2, z))
        fz0 = w0 * jnp.where(w0 > 0, at(al, x + 1, z, -1), a)
        fz1 = w1 * jnp.where(w1 > 0, a, at(al, x + 1, z, 1))
        new = a - 0.2 * (fx1 - fx0 + fz1 - fz0)
        to_out(an_s, x, z, new)
        rho[x + 1, :, pl.ds(ROW0 + z * 8, 8), :] = 1.0 + 9.0 * new

    def first(x, z):
        d = at(rho, x + 1, z)
        c = (
            recip(d + at(rho, x, z)), recip(d + at(rho, x + 2, z)),
            recip(d + at(rho, x + 1, z, -1)), recip(d + at(rho, x + 1, z, 1)),
            recip(d + y_minus(d)), recip(d + y_plus(d)),
        )
        inv = recip(c[0] + c[1] + c[2] + c[3] + c[4] + c[5])
        c = [v * inv for v in c]
        r = 0.5 * raw(div, x, z) * inv
        for ref, v in zip((axm, axp, azm, azp, aym, ayp, rr), c + [r]):
            ref[x, :, pl.ds(z * 8, 8), :] = v
        return apply(p0, c, r, x, z)

    def apply(p, c, r, x, z):
        q = at(p, x + 1, z)
        return (
            (c[0] * at(p, x, z) + c[1] * at(p, x + 2, z))
            + (c[2] * at(p, x + 1, z, -1) + c[3] * at(p, x + 1, z, 1))
            + (c[4] * y_minus(q) + c[5] * y_plus(q) - r)
        )

    def later(p, x, z):
        c = [raw(ref, x, z) for ref in (axm, axp, azm, azp, aym, ayp)]
        return apply(p, c, raw(rr, x, z), x, z)

    def sweep1(x, z):
        p1[x + 1, :, pl.ds(ROW0 + z * 8, 8), :] = first(x, z)

    def sweep2(x, z):
        p2[x + 1, :, pl.ds(ROW0 + z * 8, 8), :] = later(p1, x, z)

    def sweep3(x, z):
        to_out(pr_s, x, z, later(p2, x, z))

    tiles = CZ // 8

    def interior(fn, zs_):
        def step(x, c):
            for z in zs_:
                fn(x, z)
            return c

        lax.fori_loop(1, CX - 1, step, 0)

    def ends(fn):
        def step(z, c):
            fn(0, z)
            fn(CX - 1, z)
            return c

        lax.fori_loop(0, tiles, step, 0)

    inner, edge = range(1, tiles - 1), (0, tiles - 1)

    def recv(copies):
        for c in copies:
            c.wait_recv()

    interior(advect, inner)
    recv(ez_al + ez_vz)
    fill_z([(0, al, 1, ROW0 - 1, 0), (1, al, 1, ROW0 + CZ, DEPTHS - 1), (2, vz, 0, CZ, DEPTHS - 1)])
    interior(advect, edge)
    recv(e_al + e_vx)
    zero_x(al)

    @pl.when(slab == SLABS - 1)
    def _():
        vx[CX] = jnp.zeros((NB, CZ, LANES), F32)

    ends(advect)
    e_rho, ez_rho = xpair(5, rho), zpair(5)
    start(e_rho)
    pack_z([(5, rho, 1, ROW0 + CZ - 1), (6, rho, 1, ROW0)])
    start(ez_rho)
    out_alpha = pltpu.make_async_copy(an_s, alpha_o, out_sem.at[0])
    out_alpha.start()

    def b1_wait(k, c):
        src = (b_me + GB - k) % GB
        rcopy(s1.at[src], r1.at[src], b1s.at[k], b1r.at[k], b_peer(k)[1]).wait_recv()
        return c

    lax.fori_loop(1, GB, b1_wait, 0)
    pr, pc = iota((SLOTS, SLOTS), 0), iota((SLOTS, SLOTS), 1)
    perm_s[...] = onehot(
        pc == (((pr >> 2) & (GB - 1)) * REC_B + (pr >> 6) * CAP + (pr & 3))
    )
    got = dot(perm_s[...], r1[:, 0:REC_B, :].reshape(SLOTS, LANES)).astype(BF16)
    brow = iota((META, LANES), 0)
    m1 = jnp.zeros((META, LANES), F32)
    for b in range(GB):
        m1 = jnp.where(brow == b, r1[b, REC_B:, :].astype(F32), m1)
    m1 = m1.astype(BF16)
    for a in range(GA):
        s2[a, 0:REC_A, :] = got[a * REC_A : (a + 1) * REC_A]
        s2[a, REC_A:, :] = m1

    def a1_copy(k):
        a, dev = a_peer(k)
        return rcopy(s2.at[a], r2.at[a_me], a1s.at[k], a1r.at[k], dev)

    def a1_start(k, c):
        a1_copy(k).start()
        return c

    lax.fori_loop(1, GA, a1_start, 0)
    r2[a_me] = s2[a_me]
    perm_s[...] = onehot(
        pc == (((pr >> 2) & (GA - 1)) * REC_A + (pr >> 5) * CAP + (pr & 3))
    )
    for c in loads["div"]:
        c.wait()

    def a1_wait(k, c):
        src = (a_me + GA - k) % GA
        rcopy(s2.at[src], r2.at[src], a1s.at[k], a1r.at[k], a_peer(k)[1]).wait_recv()
        return c

    lax.fori_loop(1, GA, a1_wait, 0)

    m2 = r2[:, REC_A:, :].reshape(GA * GB, LANES)
    wide = dot(onehot((iota((SLOTS, LANES), 0) >> 2) == iota((SLOTS, LANES), 1)), m2)
    pick = iota((SLOTS, LANES), 1) - (iota((SLOTS, LANES), 0) & 3) - a_me * CAP
    hi_c = jnp.sum(jnp.where(pick == 0, wide, 0.0), axis=1, keepdims=True)
    lo_c = jnp.sum(jnp.where(pick == REC_B, wide, 0.0), axis=1, keepdims=True)
    seg_c = hi_c.astype(I32) * 64 + lo_c.astype(I32)
    block_c, key_c = seg_c & 3, seg_c >> 2
    key_f = jnp.broadcast_to(key_c, (SLOTS, LANES)).astype(F32)
    key_r = key_f.T[0:1]
    for c in range(CX * CZ // LANES):
        g_s[:, c * LANES : (c + 1) * LANES] = onehot(
            key_f == (iota((SLOTS, LANES), 1) + c * LANES).astype(F32)
        )
    recs = r2[:, 0:REC_A, :].reshape(SLOTS, LANES)
    for y in range(NB):
        rmat[:, y * LANES : (y + 1) * LANES] = jnp.where(
            block_c == y, recs.astype(F32), 0.0
        ).astype(BF16)

    def hull(x, c):
        cells = (iota((CZ, SLOTS), 0) + x * CZ).astype(F32)
        h = dot(onehot(cells == key_r), rmat[...])
        for y in range(NB):
            div[x, y] += h[:, y * LANES : (y + 1) * LANES]
        return c

    lax.fori_loop(0, CX, hull, 0)

    interior(sweep1, inner)
    recv(ez_p0 + ez_rho)
    fill_z([
        (3, p0, 1, ROW0 - 1, 0), (4, p0, 1, ROW0 + CZ, DEPTHS - 1),
        (5, rho, 1, ROW0 - 1, 0), (6, rho, 1, ROW0 + CZ, DEPTHS - 1),
    ])
    interior(sweep1, edge)
    recv(e_p0 + e_rho)
    zero_x(p0)
    zero_x(rho)
    ends(sweep1)
    e_p1, ez_p1 = xpair(7, p1), zpair(7)
    start(e_p1)
    pack_z([(7, p1, 1, ROW0 + CZ - 1), (8, p1, 1, ROW0)])
    start(ez_p1)
    interior(sweep2, inner)
    recv(ez_p1)
    fill_z([(7, p1, 1, ROW0 - 1, 0), (8, p1, 1, ROW0 + CZ, DEPTHS - 1)])
    interior(sweep2, edge)
    recv(e_p1)
    zero_x(p1)
    ends(sweep2)
    e_p2, ez_p2 = xpair(9, p2), zpair(9)
    start(e_p2)
    pack_z([(9, p2, 1, ROW0 + CZ - 1), (10, p2, 1, ROW0)])
    start(ez_p2)
    interior(sweep3, inner)
    recv(ez_p2)
    fill_z([(9, p2, 1, ROW0 - 1, 0), (10, p2, 1, ROW0 + CZ, DEPTHS - 1)])
    interior(sweep3, edge)
    recv(e_p2)
    zero_x(p2)
    ends(sweep3)
    out_press = pltpu.make_async_copy(pr_s, press_o, out_sem.at[1])
    out_press.start()

    for x in range(CX):
        pb[x * CZ : (x + 1) * CZ, :] = pr_s[x].astype(BF16)
    wet = dot(g_s[...], pb[...])
    back = jnp.zeros((SLOTS, LANES), F32)
    for y in range(NB):
        back = jnp.where(block_c == y, wet[:, y * LANES : (y + 1) * LANES], back)
    back = back.astype(BF16)
    for a in range(GA):
        s3[a] = back[a * REC_A : (a + 1) * REC_A]

    def a2_start(k, c):
        a, dev = a_peer(k)
        rcopy(s3.at[a], t1.at[a_me], a2s.at[k], a2r.at[k], dev).start()
        return c

    def a2_wait(k, c):
        src = (a_me + GA - k) % GA
        rcopy(s3.at[src], t1.at[src], a2s.at[k], a2r.at[k], a_peer(k)[1]).wait_recv()
        return c

    lax.fori_loop(1, GA, a2_start, 0)
    t1[a_me] = s3[a_me]
    lax.fori_loop(1, GA, a2_wait, 0)
    turned = dot(perm_s[...], t1[...].reshape(SLOTS, LANES)).astype(BF16)
    for b in range(GB):
        s4[b] = turned[b * REC_B : (b + 1) * REC_B]

    def b2_start(k, c):
        b, dev = b_peer(k)
        rcopy(s4.at[b], t2.at[b_me], b2s.at[k], b2r.at[k], dev).start()
        return c

    def b2_wait(k, c):
        src = (b_me + GB - k) % GB
        rcopy(s4.at[src], t2.at[src], b2s.at[k], b2r.at[k], b_peer(k)[1]).wait_recv()
        return c

    lax.fori_loop(1, GB, b2_start, 0)
    t2[b_me] = s4[b_me]
    lax.fori_loop(1, GB, b2_wait, 0)
    panel_o[...] = dot(q_s[...], t2[...].reshape(SLOTS, LANES)).astype(BF16)

    for c in sends:
        c.wait_send()

    def b_done(k, c):
        b, dev = b_peer(k)
        rcopy(s1.at[b], r1.at[b_me], b1s.at[k], b1r.at[k], dev).wait_send()
        rcopy(s4.at[b], t2.at[b_me], b2s.at[k], b2r.at[k], dev).wait_send()
        return c

    def a_done(k, c):
        a, dev = a_peer(k)
        rcopy(s2.at[a], r2.at[a_me], a1s.at[k], a1r.at[k], dev).wait_send()
        rcopy(s3.at[a], t1.at[a_me], a2s.at[k], a2r.at[k], dev).wait_send()
        return c

    lax.fori_loop(1, GB, b_done, 0)
    lax.fori_loop(1, GA, a_done, 0)
    out_alpha.wait()
    out_press.wait()


def body(alpha, vel_x, vel_z, divergence, press_guess, panel_records, panel_dest, panel_segment):
    padded = pltpu.VMEM((CX + 2, NB, PADZ, LANES), F32)
    plain = pltpu.VMEM((CX, NB, CZ, LANES), F32)
    natural = pltpu.VMEM((CX, CZ, BEAM), F32)
    hbm = pl.BlockSpec(memory_space=pl.ANY)
    vmem = pl.BlockSpec(memory_space=pltpu.VMEM)
    dma = lambda n: pltpu.SemaphoreType.DMA((n,))
    field = jax.ShapeDtypeStruct((CX, CZ, BEAM), F32)
    return pl.pallas_call(
        kernel,
        out_shape=(field, field, jax.ShapeDtypeStruct((PAN, LANES), BF16)),
        in_specs=[hbm] * 5 + [vmem] * 3,
        out_specs=(hbm, hbm, vmem),
        scratch_shapes=[
            padded,
            pltpu.VMEM((CX + 1, NB, CZ, LANES), F32),
            pltpu.VMEM((CX, NB, CZ + 8, LANES), F32),
            plain,
            padded, padded, padded, padded,
            natural, natural,
            plain, plain, plain, plain, plain, plain, plain,
            pltpu.VMEM((11, CX, NB, LANES), F32),
            pltpu.VMEM((11, CX, NB, LANES), F32),
            pltpu.VMEM((GB, REC_B + META, LANES), BF16),
            pltpu.VMEM((GB, REC_B + META, LANES), BF16),
            pltpu.VMEM((GA, REC_A + META, LANES), BF16),
            pltpu.VMEM((GA, REC_A + META, LANES), BF16),
            pltpu.VMEM((GA, REC_A, LANES), BF16),
            pltpu.VMEM((GA, REC_A, LANES), BF16),
            pltpu.VMEM((GB, REC_B, LANES), BF16),
            pltpu.VMEM((GB, REC_B, LANES), BF16),
            pltpu.VMEM((PAN, SLOTS), BF16),
            pltpu.VMEM((SLOTS, CX * CZ), BF16),
            pltpu.VMEM((SLOTS, SLOTS), BF16),
            pltpu.VMEM((SLOTS, BEAM), BF16),
            pltpu.VMEM((CX * CZ, BEAM), BF16),
            dma(20), dma(2), dma(11), dma(11), dma(11), dma(11),
            dma(GB), dma(GB), dma(GA), dma(GA), dma(GA), dma(GA), dma(GB), dma(GB),
        ],
        compiler_params=pltpu.CompilerParams(
            collective_id=0, has_side_effects=True, vmem_limit_bytes=60 * 1024 * 1024
        ),
    )(
        alpha, vel_x, vel_z, divergence, press_guess, panel_records,
        panel_dest.reshape(1, PAN), panel_segment.reshape(1, PAN),
    )


def solution(mesh):
    field = P("slab", "depth", None)
    rows = P(("slab", "depth"), None)
    return jax.shard_map(
        body, mesh=mesh, in_specs=(field,) * 5 + (rows,) * 3,
        out_specs=(field, field, rows), check_vma=False,
    )
```

time: 201 us -> 63 us (0.31)
  starting transfers between devices: 83.7 us -> 0 us
  other arithmetic: 58.5 us -> 0 us
  Pallas kernels: 0 us -> 56.8 us
  waiting for transfers between devices: 39 us -> 0 us
  local copies, waits for them, and re-layouts: 17.7 us -> 5.25 us
    pallas_call x0 -> x1, Pallas kernels: none -> 56.8 us  [body(): pl.pallas_call(kernel, out_shape=(field, field, jax.ShapeDtypeStruct((PAN...]
    ppermute x20 -> x0, starting transfers between devices: 51.1 us -> none  [the longest x10 34.6 us: with_halo(): lax.ppermute(lax.slice_in_dim(block, block.shape[dim] - width, None, axis...]
    all_to_all x3 -> x0, starting transfers between devices: 32.6 us -> none  [the longest x1 12.4 us: body(): lax.all_to_all(wall_rows, ('slab', 'depth'), split_axis=0, concat_axis=0,...]
    div x2 -> x0, other arithmetic: 22.6 us -> none  [sweep(): return (total - rhs) / weight]
    ppermute x20 -> x0, waiting for transfers between devices: 20.5 us -> none  [the longest x10 19.2 us: with_halo(): lax.ppermute(lax.slice_in_dim(block, 0, width, axis=dim), axis, backward)]
    all_to_all x3 -> x0, waiting for transfers between devices: 18.5 us -> none  [the longest x1 9.83 us: body(): lax.all_to_all(wall_rows, ('slab', 'depth'), split_axis=0, concat_axis=0,...]
    concatenate x6 -> x0, other arithmetic: 15.9 us -> none  [with_halo(): block = jnp.concatenate([low, block, high], axis=dim)]
    convert_element_type x1 -> x0, other arithmetic: 10.5 us -> none  [body(): wall_rows = pressure.reshape(-1, 128).astype(jnp.bfloat16)[got_seg]]
  transfers between devices with their start and end apart: 23 -> 0, of which waited for: 9 -> 0; matrix products, arithmetic and copies ran while one was open for 10% -> 0% of each run, Pallas kernels for 0% -> 0%
where the time goes in v1:
time: 63 us; the launch traced here: 62.7 us
  Pallas kernels  56.8 us (90%)
  local copies, waits for them, and re-layouts  5.25 us (8%)
  between operations  0.65 us (1%)
    pallas_call x1, Pallas kernels, body(): pl.pallas_call(kernel, out_shape=(field, field, jax.ShapeDtypeStruct((PAN...  56.8 us
    unnamed x7, local copies, waits for them, and re-layouts  5.25 us

profile of v1, /device:TPU:1, one launch (start us, length us, event | category | flops | bytes accessed | tf_op | source)
XLA Modules:
  0.0 62.7 jit_solution(14115624577007963698)
XLA Ops:
  0.6 56.8 %shard_map.103 = (f32[16,64,512]{2,1,0:T(8,128)}, f32[16,64,512]{2,1,0:T(8,128)}, bf16[256,128]{1,0:T(8,128)(2,1)}) custom-call(f32[16,64,512]{2,1,0:T(8,128)} %alpha_h.1, f32[16,64,512]{2,1,0:T(8,128)} %velx_h.1, f32[16,64,512]{2,1,0:T(8,128)} %velz_h.1, f32[16,64,512]{2,1,0:T(8,128)} %div_h.1, f32[16,64,512]{2,1,0:T(8,128)} %press_h.1, ...), custom_call_target="tpu_custom_call" | custom-call | tf_op jit(solution)/shard_map/pallas_call | solution.py:493
  57.4 0.0 copy-start
  57.5 3.3 %copy.14 = f32[16,64,512]{2,1,0:T(8,128)} copy(f32[16,64,512]{2,1,0:T(8,128)} %get-tuple-element.6) | data formatting | bytes 4194304
  60.8 0.0 copy-done
  60.8 0.0 copy-start.1
  60.8 1.3 %copy.15 = f32[16,64,512]{2,1,0:T(8,128)} copy(f32[16,64,512]{2,1,0:T(8,128)S(1)} %copy-done) | data formatting | bytes 4194304
  62.1 0.0 copy-done.1
  62.1 0.6 %copy.16 = bf16[256,128]{1,0:T(8,128)(2,1)} copy(bf16[256,128]{1,0:T(8,128)(2,1)S(1)} %copy-done.1) | data formatting | bytes 131072
Async XLA Ops:
  57.4 3.3 %copy-start = (f32[16,64,512]{2,1,0:T(8,128)S(1)}, f32[16,64,512]{2,1,0:T(8,128)}, u32[]{:S(2)}) copy-start(f32[16,64,512]{2,1,0:T(8,128)} %get-tuple-element.7) | copy-start | bytes 6291460
  60.8 1.3 %copy-start.1 = (bf16[256,128]{1,0:T(8,128)(2,1)S(1)}, bf16[256,128]{1,0:T(8,128)(2,1)}, u32[]{:S(2)}) copy-start(bf16[256,128]{1,0:T(8,128)(2,1)} %get-tuple-element.8) | copy-start | bytes 196612

commit v2 on v1

v2 whole, which is shorter than its diff:
```python
import jax
import jax.numpy as jnp
from jax import lax
from jax.experimental import pallas as pl
from jax.experimental.pallas import tpu as pltpu
from jax.sharding import PartitionSpec as P

MESH = pl.DeviceIdType.MESH
F32, BF16, I32 = jnp.float32, jnp.bfloat16, jnp.int32
CX, CZ, BEAM, LANES = 16, 64, 512, 128
NB = BEAM // LANES
ROW0 = 8
PADZ = CZ + 16
SLABS, DEPTHS = 32, 4
GA, GB = 8, 16
CAP = 4
SLOTS = GA * GB * CAP
PAN = 256
REC_B, REC_A = GA * CAP, GB * CAP
META = 16


def iota(shape, dim):
    return lax.broadcasted_iota(I32, shape, dim)


def onehot(cond):
    return jnp.where(cond, 1.0, 0.0).astype(BF16)


def dot(a, b):
    return jnp.dot(a, b, preferred_element_type=F32)


def recip(d):
    r = pl.reciprocal(d, approx=True)
    return r * (2.0 - d * r)


def kernel(
    alpha_h, velx_h, velz_h, div_h, press_h, rec_ref, dest_ref, seg_ref,
    press_o, alpha_o, panel_o,
    al, vx, vz, div, rho, p0, p1, p2,
    axm, axp, azm, azp, aym, ayp, rr,
    zs, zr,
    s1, r1, s2, r2, s3, t1, s4, t2,
    q_s, g_s, perm_s, rmat, pb,
    load_sem, xs_sem, xr_sem, zs_sem, zr_sem,
    b1s, b1r, a1s, a1r, a2s, a2r, b2s, b2r,
):
    slab = lax.axis_index("slab")
    depth = lax.axis_index("depth")
    up_s, dn_s = (slab + 1) % SLABS, (slab + SLABS - 1) % SLABS
    up_d, dn_d = (depth + 1) % DEPTHS, (depth + DEPTHS - 1) % DEPTHS
    x_up, x_dn = (up_s, depth), (dn_s, depth)
    z_up, z_dn = (slab, up_d), (slab, dn_d)
    b_me, core = slab // 2, slab % 2
    a_me = core * DEPTHS + depth

    def b_peer(k):
        b = (b_me + k) % GB
        return b, (b * 2 + core, depth)

    def a_peer(k):
        a = (a_me + k) % GA
        return a, (b_me * 2 + a // DEPTHS, a % DEPTHS)

    loads = {}
    sem_i = 0
    for name, src, dst in (
        ("al", alpha_h, lambda y: al.at[pl.ds(1, CX), y, pl.ds(ROW0, CZ), :]),
        ("vx", velx_h, lambda y: vx.at[pl.ds(0, CX), y, :, :]),
        ("vz", velz_h, lambda y: vz.at[:, y, pl.ds(0, CZ), :]),
        ("p0", press_h, lambda y: p0.at[pl.ds(1, CX), y, pl.ds(ROW0, CZ), :]),
        ("div", div_h, lambda y: div.at[:, y, :, :]),
    ):
        loads[name] = []
        for y in range(NB):
            c = pltpu.make_async_copy(
                src.at[:, :, pl.ds(y * LANES, LANES)], dst(y), load_sem.at[sem_i]
            )
            c.start()
            sem_i += 1
            loads[name].append(c)

    barrier = pltpu.get_barrier_semaphore()
    for dev in (x_up, x_dn, z_up, z_dn):
        pl.semaphore_signal(barrier, inc=1, device_id=dev, device_id_type=MESH)

    def sig_b(k, c):
        pl.semaphore_signal(barrier, inc=1, device_id=b_peer(k)[1], device_id_type=MESH)
        return c

    def sig_a(k, c):
        pl.semaphore_signal(barrier, inc=1, device_id=a_peer(k)[1], device_id_type=MESH)
        return c

    lax.fori_loop(1, GB, sig_b, 0)
    lax.fori_loop(1, GA, sig_a, 0)

    dest, seg = dest_ref[...], seg_ref[...]
    own = onehot(iota((GA * GB, PAN), 0) == dest)
    before = dot(own, onehot(iota((PAN, PAN), 0) < iota((PAN, PAN), 1)))
    slot = jnp.sum(own.astype(F32) * before, axis=0, keepdims=True)
    lane_of = (dest >> 3) * CAP + slot.astype(I32)
    place = (dest & (GA - 1)) * REC_A + lane_of
    packed = dot(onehot(iota((SLOTS, PAN), 0) == place), rec_ref[...]).astype(BF16)
    row = iota((LANES, PAN), 0)
    hi, lo = (seg >> 6).astype(F32), (seg & 63).astype(F32)
    bt = jnp.where(row == lane_of, hi, 0.0) + jnp.where(row == lane_of + REC_A, lo, 0.0)
    meta = lax.dot_general(
        onehot(iota((16, PAN), 0) == (dest & (GA - 1))), bt.astype(BF16),
        (((1,), (1,)), ((), ())), preferred_element_type=F32,
    )
    for a in range(GA):
        s1[a, 0:REC_A, :] = packed[a * REC_A : (a + 1) * REC_A]
        s1[a, REC_A:, :] = jnp.broadcast_to(meta[a : a + 1], (META, LANES)).astype(BF16)

    def rcopy(src, dst, ss, rs, dev):
        return pltpu.make_async_remote_copy(
            src_ref=src, dst_ref=dst, send_sem=ss, recv_sem=rs,
            device_id=dev, device_id_type=MESH,
        )

    def xcopy(i, src, src_x, dst_x, dev, padded=True):
        rows = pl.ds(ROW0, CZ) if padded else pl.ds(0, CZ)
        return rcopy(
            src.at[src_x, :, rows, :], src.at[dst_x, :, rows, :], xs_sem.at[i], xr_sem.at[i], dev
        )

    def zcopy(i, dev):
        return rcopy(zs.at[i], zr.at[i], zs_sem.at[i], zr_sem.at[i], dev)

    def xpair(i, ref):
        return [xcopy(i, ref, CX, 0, x_up), xcopy(i + 1, ref, 1, CX + 1, x_dn)]

    def zpair(i):
        return [zcopy(i, z_up), zcopy(i + 1, z_dn)]

    def pack_z(items):
        def step(g, c):
            for k in range(4):
                x = g * 4 + k
                for i, ref, xo, r in items:
                    zs[i, x] = ref[x + xo, :, r, :]
            return c

        lax.fori_loop(0, CX // 4, step, 0)

    def fill_z(items):
        def step(g, c):
            for k in range(4):
                x = g * 4 + k
                for i, ref, xo, r, edge in items:
                    ref[x + xo, :, r, :] = jnp.where(depth == edge, 0.0, zr[i, x])
            return c

        lax.fori_loop(0, CX // 4, step, 0)

    def zero_x(ref):
        @pl.when(slab == 0)
        def _():
            ref[0, :, ROW0 : ROW0 + CZ, :] = jnp.zeros((NB, CZ, LANES), F32)

        @pl.when(slab == SLABS - 1)
        def _():
            ref[CX + 1, :, ROW0 : ROW0 + CZ, :] = jnp.zeros((NB, CZ, LANES), F32)

    sends = []

    def start(copies):
        for c in copies:
            c.start()
        sends.extend(copies)

    for name in ("al", "vx", "vz"):
        for c in loads[name]:
            c.wait()
    pack_z([(0, al, 1, ROW0 + CZ - 1), (1, al, 1, ROW0), (2, vz, 0, 0)])
    pl.semaphore_wait(barrier, 4 + (GB - 1) + (GA - 1))
    e_al, e_vx = xpair(0, al), [xcopy(2, vx, 0, CX, x_dn, padded=False)]
    ez_al, ez_vz = zpair(0), [zcopy(2, z_dn)]
    start(e_al + e_vx + ez_al + ez_vz)

    def a1_start(k, c):
        a, dev = a_peer(k)
        rcopy(s1.at[a], r1.at[a_me], a1s.at[k], a1r.at[k], dev).start()
        return c

    lax.fori_loop(1, GA, a1_start, 0)
    r1[a_me] = s1[a_me]

    for c in loads["p0"]:
        c.wait()
    pack_z([(3, p0, 1, ROW0 + CZ - 1), (4, p0, 1, ROW0)])
    e_p0, ez_p0 = xpair(3, p0), zpair(3)
    start(e_p0 + ez_p0)

    place_t = jnp.broadcast_to(place.astype(F32), (LANES, PAN)).T
    for c in range(SLOTS // LANES):
        q_s[:, c * LANES : (c + 1) * LANES] = onehot(
            place_t == (iota((PAN, LANES), 1) + c * LANES).astype(F32)
        )
    pr, pc = iota((SLOTS, SLOTS), 0), iota((SLOTS, SLOTS), 1)
    perm_s[...] = onehot(
        pc == (((pr >> 2) & (GA - 1)) * REC_A + (pr >> 5) * CAP + (pr & 3))
    )

    lane = iota((NB, 8, LANES), 2)
    last = (lane == LANES - 1) & (iota((NB, 8, LANES), 0) == NB - 1)
    zero1 = jnp.zeros((1, 8, LANES), F32)

    def y_minus(v):
        r = pltpu.roll(v, 1, 2)
        return jnp.where(lane == 0, jnp.concatenate([zero1, r[: NB - 1]], axis=0), r)

    def y_plus(v):
        r = pltpu.roll(v, LANES - 1, 2)
        return jnp.where(lane == LANES - 1, jnp.concatenate([r[1:], zero1], axis=0), r)

    def at(ref, x, z, shift=0):
        return ref[x, :, pl.ds(ROW0 + z * 8 + shift, 8), :]

    def raw(ref, x, z, shift=0):
        return ref[x, :, pl.ds(z * 8 + shift, 8), :]

    def to_out(ref, x, z, v):
        for y in range(NB):
            ref[x, pl.ds(z * 8, 8), y * LANES : (y + 1) * LANES] = v[y]

    def advect(xs, z):
        a, right, fx1, u1 = at(al, xs[0] + 1, z), None, None, None
        left, u0 = at(al, xs[0], z), raw(vx, xs[0], z)
        fx0 = u0 * jnp.where(u0 > 0, left, a)
        for x in xs:
            right, u1 = at(al, x + 2, z), raw(vx, x + 1, z)
            w0, w1 = raw(vz, x, z), raw(vz, x, z, 1)
            fx1 = u1 * jnp.where(u1 > 0, a, right)
            fz0 = w0 * jnp.where(w0 > 0, at(al, x + 1, z, -1), a)
            fz1 = w1 * jnp.where(w1 > 0, a, at(al, x + 1, z, 1))
            new = a - 0.2 * (fx1 - fx0 + fz1 - fz0)
            to_out(alpha_o, x, z, new)
            rho[x + 1, :, pl.ds(ROW0 + z * 8, 8), :] = 1.0 + 9.0 * new
            a, fx0 = right, fx1

    def coefficients(xs, z):
        d = at(rho, xs[0] + 1, z)
        cm = recip(d + at(rho, xs[0], z))
        for x in xs:
            right = at(rho, x + 2, z)
            cp = recip(d + right)
            zm, zp = recip(d + at(rho, x + 1, z, -1)), recip(d + at(rho, x + 1, z, 1))
            ym = recip(d + y_minus(d))
            yp = y_plus(ym)
            yp = jnp.where(last, recip(d), yp)
            inv = recip((cm + cp) + (zm + zp) + (ym + yp))
            for ref, v in zip((axm, axp, azm, azp, aym, ayp), (cm, cp, zm, zp, ym, yp)):
                ref[x, :, pl.ds(z * 8, 8), :] = v * inv
            rr[x, :, pl.ds(z * 8, 8), :] = 0.5 * inv
            d, cm = right, cp

    def sweep(p, store, xs, z):
        left, mid = at(p, xs[0], z), at(p, xs[0] + 1, z)
        for x in xs:
            right = at(p, x + 2, z)
            store(
                x, z,
                (raw(axm, x, z) * left + raw(axp, x, z) * right)
                + (raw(azm, x, z) * at(p, x + 1, z, -1) + raw(azp, x, z) * at(p, x + 1, z, 1))
                + (raw(aym, x, z) * y_minus(mid) + raw(ayp, x, z) * y_plus(mid) - raw(rr, x, z)),
            )
            left, mid = mid, right

    def into(ref):
        def store(x, z, v):
            ref[x + 1, :, pl.ds(ROW0 + z * 8, 8), :] = v

        return store

    def sweep1(xs, z):
        sweep(p0, into(p1), xs, z)

    def sweep2(xs, z):
        sweep(p1, into(p2), xs, z)

    def sweep3(xs, z):
        sweep(p2, lambda x, z, v: to_out(press_o, x, z, v), xs, z)

    tiles = CZ // 8
    middle = tuple(range(1, CX - 1))

    def interior(fn, first, count):
        def step(i, c):
            fn(middle, first + i)
            return c

        lax.fori_loop(0, count, step, 0)

    def edges(fn):
        def step(i, c):
            fn(middle, i * (tiles - 1))
            return c

        lax.fori_loop(0, 2, step, 0)

    def ends(fn):
        def step(i, c):
            for k in range(4):
                fn((0,), i * 4 + k)
                fn((CX - 1,), i * 4 + k)
            return c

        lax.fori_loop(0, tiles // 4, step, 0)

    inside = tiles - 2

    def recv(copies):
        for c in copies:
            c.wait_recv()

    interior(advect, 1, inside)
    recv(ez_al + ez_vz)
    fill_z([(0, al, 1, ROW0 - 1, 0), (1, al, 1, ROW0 + CZ, DEPTHS - 1), (2, vz, 0, CZ, DEPTHS - 1)])
    edges(advect)

    def a1_wait(k, c):
        src = (a_me + GA - k) % GA
        rcopy(s1.at[src], r1.at[src], a1s.at[k], a1r.at[k], a_peer(k)[1]).wait_recv()
        return c

    lax.fori_loop(1, GA, a1_wait, 0)
    got = dot(perm_s[...], r1[:, 0:REC_A, :].reshape(SLOTS, LANES)).astype(BF16)
    perm_s[...] = onehot(
        pc == (((pr >> 2) & (GB - 1)) * REC_B + (pr >> 6) * CAP + (pr & 3))
    )
    mrow = iota((META, LANES), 0)
    m1 = jnp.zeros((META, LANES), F32)
    for a in range(GA):
        m1 = jnp.where(mrow == a, r1[a, REC_A:, :].astype(F32), m1)
    m1 = m1.astype(BF16)
    for b in range(GB):
        s2[b, 0:REC_B, :] = got[b * REC_B : (b + 1) * REC_B]
        s2[b, REC_B:, :] = m1

    recv(e_al + e_vx)
    zero_x(al)

    @pl.when(slab == SLABS - 1)
    def _():
        vx[CX] = jnp.zeros((NB, CZ, LANES), F32)

    ends(advect)
    e_rho, ez_rho = xpair(5, rho), zpair(5)
    start(e_rho)
    pack_z([(5, rho, 1, ROW0 + CZ - 1), (6, rho, 1, ROW0)])
    start(ez_rho)

    def b1_start(k, c):
        b, dev = b_peer(k)
        rcopy(s2.at[b], r2.at[b_me], b1s.at[k], b1r.at[k], dev).start()
        return c

    lax.fori_loop(1, GB, b1_start, 0)
    r2[b_me] = s2[b_me]

    interior(coefficients, 1, inside)
    recv(ez_p0 + ez_rho)
    fill_z([
        (3, p0, 1, ROW0 - 1, 0), (4, p0, 1, ROW0 + CZ, DEPTHS - 1),
        (5, rho, 1, ROW0 - 1, 0), (6, rho, 1, ROW0 + CZ, DEPTHS - 1),
    ])
    edges(coefficients)
    recv(e_p0 + e_rho)
    zero_x(p0)
    zero_x(rho)
    ends(coefficients)
    for c in loads["div"]:
        c.wait()

    def b1_wait(k, c):
        src = (b_me + GB - k) % GB
        rcopy(s2.at[src], r2.at[src], b1s.at[k], b1r.at[k], b_peer(k)[1]).wait_recv()
        return c

    lax.fori_loop(1, GB, b1_wait, 0)

    m2 = r2[:, REC_B:, :].reshape(GB * META, LANES)
    srow, scol = iota((SLOTS, GB * META), 0), iota((SLOTS, GB * META), 1)
    wide = dot(onehot(scol == (srow >> 5) * META + ((srow >> 2) & (GA - 1))), m2)
    pick = iota((SLOTS, LANES), 1) - (iota((SLOTS, LANES), 0) & 3) - b_me * CAP
    hi_c = jnp.sum(jnp.where(pick == 0, wide, 0.0), axis=1, keepdims=True)
    lo_c = jnp.sum(jnp.where(pick == REC_A, wide, 0.0), axis=1, keepdims=True)
    seg_c = hi_c.astype(I32) * 64 + lo_c.astype(I32)
    block_c, key_c = seg_c & 3, seg_c >> 2
    key_f = jnp.broadcast_to(key_c, (SLOTS, LANES)).astype(F32)
    key_r = key_f.T[0:1]
    recs = r2[:, 0:REC_B, :].reshape(SLOTS, LANES)
    for y in range(NB):
        rmat[:, y * LANES : (y + 1) * LANES] = jnp.where(
            block_c == y, recs.astype(F32), 0.0
        ).astype(BF16)

    def hull(i, c):
        cells = (iota((4 * CZ, SLOTS), 0) + i * (4 * CZ)).astype(F32)
        h = dot(onehot(cells == key_r), rmat[...])
        for k in range(4):
            x = i * 4 + k
            for y in range(NB):
                part = h[k * CZ : (k + 1) * CZ, y * LANES : (y + 1) * LANES]
                rr[x, y] = (div[x, y] + part) * rr[x, y]
        return c

    lax.fori_loop(0, CX // 4, hull, 0)

    ends(sweep1)
    e_p1, ez_p1 = xpair(7, p1), zpair(7)
    start(e_p1)
    edges(sweep1)
    pack_z([(7, p1, 1, ROW0 + CZ - 1), (8, p1, 1, ROW0)])
    start(ez_p1)
    interior(sweep1, 1, inside)
    for c in range(CX * CZ // LANES):
        g_s[:, c * LANES : (c + 1) * LANES] = onehot(
            key_f == (iota((SLOTS, LANES), 1) + c * LANES).astype(F32)
        )
    interior(sweep2, 1, inside // 2)
    recv(ez_p1)
    fill_z([(7, p1, 1, ROW0 - 1, 0), (8, p1, 1, ROW0 + CZ, DEPTHS - 1)])
    recv(e_p1)
    zero_x(p1)
    ends(sweep2)
    e_p2, ez_p2 = xpair(9, p2), zpair(9)
    start(e_p2)
    edges(sweep2)
    pack_z([(9, p2, 1, ROW0 + CZ - 1), (10, p2, 1, ROW0)])
    start(ez_p2)
    interior(sweep2, 1 + inside // 2, inside - inside // 2)
    interior(sweep3, 1, inside)
    recv(ez_p2)
    fill_z([(9, p2, 1, ROW0 - 1, 0), (10, p2, 1, ROW0 + CZ, DEPTHS - 1)])
    edges(sweep3)
    recv(e_p2)
    zero_x(p2)
    ends(sweep3)

    for x in range(CX):
        pb[x * CZ : (x + 1) * CZ, :] = press_o[x].astype(BF16)
    wet = dot(g_s[...], pb[...])
    back = jnp.zeros((SLOTS, LANES), F32)
    for y in range(NB):
        back = jnp.where(block_c == y, wet[:, y * LANES : (y + 1) * LANES], back)
    back = back.astype(BF16)
    for b in range(GB):
        s3[b] = back[b * REC_B : (b + 1) * REC_B]

    def b2_start(k, c):
        b, dev = b_peer(k)
        rcopy(s3.at[b], t1.at[b_me], b2s.at[k], b2r.at[k], dev).start()
        return c

    def b2_wait(k, c):
        src = (b_me + GB - k) % GB
        rcopy(s3.at[src], t1.at[src], b2s.at[k], b2r.at[k], b_peer(k)[1]).wait_recv()
        return c

    lax.fori_loop(1, GB, b2_start, 0)
    t1[b_me] = s3[b_me]
    lax.fori_loop(1, GB, b2_wait, 0)
    turned = dot(perm_s[...], t1[...].reshape(SLOTS, LANES)).astype(BF16)
    for a in range(GA):
        s4[a] = turned[a * REC_A : (a + 1) * REC_A]

    def a2_start(k, c):
        a, dev = a_peer(k)
        rcopy(s4.at[a], t2.at[a_me], a2s.at[k], a2r.at[k], dev).start()
        return c

    def a2_wait(k, c):
        src = (a_me + GA - k) % GA
        rcopy(s4.at[src], t2.at[src], a2s.at[k], a2r.at[k], a_peer(k)[1]).wait_recv()
        return c

    lax.fori_loop(1, GA, a2_start, 0)
    t2[a_me] = s4[a_me]
    lax.fori_loop(1, GA, a2_wait, 0)
    panel_o[...] = dot(q_s[...], t2[...].reshape(SLOTS, LANES)).astype(BF16)

    for c in sends:
        c.wait_send()

    def b_done(k, c):
        b, dev = b_peer(k)
        rcopy(s2.at[b], r2.at[b_me], b1s.at[k], b1r.at[k], dev).wait_send()
        rcopy(s3.at[b], t1.at[b_me], b2s.at[k], b2r.at[k], dev).wait_send()
        return c

    def a_done(k, c):
        a, dev = a_peer(k)
        rcopy(s1.at[a], r1.at[a_me], a1s.at[k], a1r.at[k], dev).wait_send()
        rcopy(s4.at[a], t2.at[a_me], a2s.at[k], a2r.at[k], dev).wait_send()
        return c

    lax.fori_loop(1, GB, b_done, 0)
    lax.fori_loop(1, GA, a_done, 0)


def body(alpha, vel_x, vel_z, divergence, press_guess, panel_records, panel_dest, panel_segment):
    padded = pltpu.VMEM((CX + 2, NB, PADZ, LANES), F32)
    plain = pltpu.VMEM((CX, NB, CZ, LANES), F32)
    hbm = pl.BlockSpec(memory_space=pl.ANY)
    vmem = pl.BlockSpec(memory_space=pltpu.VMEM)
    dma = lambda n: pltpu.SemaphoreType.DMA((n,))
    field = pltpu.VMEM((CX, CZ, BEAM), F32)
    return pl.pallas_call(
        kernel,
        out_shape=(field, field, pltpu.VMEM((PAN, LANES), BF16)),
        in_specs=[hbm] * 5 + [vmem] * 3,
        out_specs=(vmem, vmem, vmem),
        scratch_shapes=[
            padded,
            pltpu.VMEM((CX + 1, NB, CZ, LANES), F32),
            pltpu.VMEM((CX, NB, CZ + 8, LANES), F32),
            plain,
            padded, padded, padded, padded,
            plain, plain, plain, plain, plain, plain, plain,
            pltpu.VMEM((11, CX, NB, LANES), F32),
            pltpu.VMEM((11, CX, NB, LANES), F32),
            pltpu.VMEM((GA, REC_A + META, LANES), BF16),
            pltpu.VMEM((GA, REC_A + META, LANES), BF16),
            pltpu.VMEM((GB, REC_B + META, LANES), BF16),
            pltpu.VMEM((GB, REC_B + META, LANES), BF16),
            pltpu.VMEM((GB, REC_B, LANES), BF16),
            pltpu.VMEM((GB, REC_B, LANES), BF16),
            pltpu.VMEM((GA, REC_A, LANES), BF16),
            pltpu.VMEM((GA, REC_A, LANES), BF16),
            pltpu.VMEM((PAN, SLOTS), BF16),
            pltpu.VMEM((SLOTS, CX * CZ), BF16),
            pltpu.VMEM((SLOTS, SLOTS), BF16),
            pltpu.VMEM((SLOTS, BEAM), BF16),
            pltpu.VMEM((CX * CZ, BEAM), BF16),
            dma(20), dma(11), dma(11), dma(11), dma(11),
            dma(GB), dma(GB), dma(GA), dma(GA), dma(GA), dma(GA), dma(GB), dma(GB),
        ],
        compiler_params=pltpu.CompilerParams(
            collective_id=0, has_side_effects=True, vmem_limit_bytes=59 * 1024 * 1024 + 768 * 1024
        ),
    )(
        alpha, vel_x, vel_z, divergence, press_guess, panel_records,
        panel_dest.reshape(1, PAN), panel_segment.reshape(1, PAN),
    )


def solution(mesh):
    field = P("slab", "depth", None)
    rows = P(("slab", "depth"), None)
    return jax.shard_map(
        body, mesh=mesh, in_specs=(field,) * 5 + (rows,) * 3,
        out_specs=(field, field, rows), check_vma=False,
    )
```

time: 63 us -> 50.5 us (0.80)
  Pallas kernels: 56.8 us -> 46.5 us
  local copies, waits for them, and re-layouts: 5.25 us -> 3.27 us
    pallas_call x1, Pallas kernels: 56.8 us -> 46.5 us  [body(): pl.pallas_call(kernel, out_shape=(field, field, pltpu.VMEM((PAN, LANES),...]
    unnamed x7 -> x3, local copies, waits for them, and re-layouts: 5.25 us -> 3.27 us
where the time goes in v2:
time: 50.5 us; the launch traced here: 50.4 us
  Pallas kernels  46.5 us (92%)
  local copies, waits for them, and re-layouts  3.27 us (6%)
  between operations  0.64 us (1%)
    pallas_call x1, Pallas kernels, body(): pl.pallas_call(kernel, out_shape=(field, field, pltpu.VMEM((PAN, LANES),...  46.5 us
    unnamed x3, local copies, waits for them, and re-layouts  3.27 us

profile of v2, /device:TPU:1, one launch (start us, length us, event | category | flops | bytes accessed | tf_op | source)
XLA Modules:
  0.0 50.4 jit_solution(7549102864269200043)
XLA Ops:
  0.6 46.5 %shard_map.103 = (f32[16,64,512]{2,1,0:T(8,128)S(1)}, f32[16,64,512]{2,1,0:T(8,128)S(1)}, bf16[256,128]{1,0:T(8,128)(2,1)S(1)}) custom-call(f32[16,64,512]{2,1,0:T(8,128)} %alpha_h.1, f32[16,64,512]{2,1,0:T(8,128)} %velx_h.1, f32[16,64,512]{2,1,0:T(8,128)} %velz_h.1, f32[16,64,512]{2,1,0:T(8,128)} %div_h.1, f32[16,64,512]{2,1,0:T(8,128)} %press_h.1, ...), custom_call_target="tpu_custom_call" | custom-call | tf_op jit(solution)/shard_map/pallas_call | solution.py:514
  47.1 1.3 %copy.14 = f32[16,64,512]{2,1,0:T(8,128)} copy(f32[16,64,512]{2,1,0:T(8,128)S(1)} %get-tuple-element.3) | data formatting | bytes 4194304
  48.4 0.6 %copy.16 = bf16[256,128]{1,0:T(8,128)(2,1)} copy(bf16[256,128]{1,0:T(8,128)(2,1)S(1)} %get-tuple-element.5) | data formatting | bytes 131072
  49.1 1.3 %copy.15 = f32[16,64,512]{2,1,0:T(8,128)} copy(f32[16,64,512]{2,1,0:T(8,128)S(1)} %get-tuple-element.4) | data formatting | bytes 4194304

commit v3 on v2

--- a/solution.py
+++ b/solution.py
@@ -38,11 +38,11 @@
 
 
 def kernel(
-    alpha_h, velx_h, velz_h, div_h, press_h, rec_ref, dest_ref, seg_ref,
+    alpha_h, velx_h, velz_h, div_h, press_h, rec_h, dest_h, seg_h,
     press_o, alpha_o, panel_o,
-    al, vx, vz, div, rho, p0, p1, p2,
+    rec_ref, dest_ref, seg_ref, al, vx, vz, div, rho, p0, p1, p2,
     axm, axp, azm, azp, aym, ayp, rr,
-    zs, zr,
+    zs, zr, xb, xr, acc,
     s1, r1, s2, r2, s3, t1, s4, t2,
     q_s, g_s, perm_s, rmat, pb,
     load_sem, xs_sem, xr_sem, zs_sem, zr_sem,
@@ -67,22 +67,30 @@
 
     loads = {}
     sem_i = 0
-    for name, src, dst in (
-        ("al", alpha_h, lambda y: al.at[pl.ds(1, CX), y, pl.ds(ROW0, CZ), :]),
-        ("vx", velx_h, lambda y: vx.at[pl.ds(0, CX), y, :, :]),
-        ("vz", velz_h, lambda y: vz.at[:, y, pl.ds(0, CZ), :]),
-        ("p0", press_h, lambda y: p0.at[pl.ds(1, CX), y, pl.ds(ROW0, CZ), :]),
-        ("div", div_h, lambda y: div.at[:, y, :, :]),
-    ):
+
+    def load(name, pairs):
+        nonlocal sem_i
         loads[name] = []
-        for y in range(NB):
-            c = pltpu.make_async_copy(
-                src.at[:, :, pl.ds(y * LANES, LANES)], dst(y), load_sem.at[sem_i]
-            )
+        for src, dst in pairs:
+            c = pltpu.make_async_copy(src, dst, load_sem.at[sem_i])
             c.start()
             sem_i += 1
             loads[name].append(c)
 
+    def loaded(name):
+        for c in loads[name]:
+            c.wait()
+
+    def field(src, dst):
+        return [(src.at[:, :, pl.ds(y * LANES, LANES)], dst(y)) for y in range(NB)]
+
+    load("panels", [(dest_h, dest_ref), (seg_h, seg_ref), (rec_h, rec_ref)])
+    load("al", field(alpha_h, lambda y: al.at[pl.ds(1, CX), y, pl.ds(ROW0, CZ), :]))
+    load("vx", field(velx_h, lambda y: vx.at[pl.ds(0, CX), y, :, :]))
+    load("vz", field(velz_h, lambda y: vz.at[:, y, pl.ds(0, CZ), :]))
+    load("p0", field(press_h, lambda y: p0.at[pl.ds(1, CX), y, pl.ds(ROW0, CZ), :]))
+    load("div", field(div_h, lambda y: div.at[:, y, :, :]))
+
     barrier = pltpu.get_barrier_semaphore()
     for dev in (x_up, x_dn, z_up, z_dn):
         pl.semaphore_signal(barrier, inc=1, device_id=dev, device_id_type=MESH)
@@ -98,6 +106,7 @@
     lax.fori_loop(1, GB, sig_b, 0)
     lax.fori_loop(1, GA, sig_a, 0)
 
+    loaded("panels")
     dest, seg = dest_ref[...], seg_ref[...]
     own = onehot(iota((GA * GB, PAN), 0) == dest)
     before = dot(own, onehot(iota((PAN, PAN), 0) < iota((PAN, PAN), 1)))
@@ -122,17 +131,23 @@
             device_id=dev, device_id_type=MESH,
         )
 
-    def xcopy(i, src, src_x, dst_x, dev, padded=True):
-        rows = pl.ds(ROW0, CZ) if padded else pl.ds(0, CZ)
-        return rcopy(
-            src.at[src_x, :, rows, :], src.at[dst_x, :, rows, :], xs_sem.at[i], xr_sem.at[i], dev
-        )
+    def xcopy(i, dev):
+        return rcopy(xb.at[i], xr.at[i], xs_sem.at[i], xr_sem.at[i], dev)
 
     def zcopy(i, dev):
         return rcopy(zs.at[i], zr.at[i], zs_sem.at[i], zr_sem.at[i], dev)
 
-    def xpair(i, ref):
-        return [xcopy(i, ref, CX, 0, x_up), xcopy(i + 1, ref, 1, CX + 1, x_dn)]
+    def xpair(i):
+        return [xcopy(i, x_up), xcopy(i + 1, x_dn)]
+
+    def pack_x(i, ref):
+        xb[i] = ref[CX, :, ROW0 : ROW0 + CZ, :].astype(BF16)
+        xb[i + 1] = ref[1, :, ROW0 : ROW0 + CZ, :].astype(BF16)
+
+    def fill_x(i, ref):
+        low, high = xr[i].astype(F32), xr[i + 1].astype(F32)
+        ref[0, :, ROW0 : ROW0 + CZ, :] = jnp.where(slab == 0, 0.0, low)
+        ref[CX + 1, :, ROW0 : ROW0 + CZ, :] = jnp.where(slab == SLABS - 1, 0.0, high)
 
     def zpair(i):
         return [zcopy(i, z_up), zcopy(i + 1, z_dn)]
@@ -157,15 +172,6 @@
 
         lax.fori_loop(0, CX // 4, step, 0)
 
-    def zero_x(ref):
-        @pl.when(slab == 0)
-        def _():
-            ref[0, :, ROW0 : ROW0 + CZ, :] = jnp.zeros((NB, CZ, LANES), F32)
-
-        @pl.when(slab == SLABS - 1)
-        def _():
-            ref[CX + 1, :, ROW0 : ROW0 + CZ, :] = jnp.zeros((NB, CZ, LANES), F32)
-
     sends = []
 
     def start(copies):
@@ -173,14 +179,18 @@
             c.start()
         sends.extend(copies)
 
-    for name in ("al", "vx", "vz"):
-        for c in loads[name]:
-            c.wait()
-    pack_z([(0, al, 1, ROW0 + CZ - 1), (1, al, 1, ROW0), (2, vz, 0, 0)])
+    loaded("al")
+    pack_x(0, al)
+    pack_z([(0, al, 1, ROW0 + CZ - 1), (1, al, 1, ROW0)])
     pl.semaphore_wait(barrier, 4 + (GB - 1) + (GA - 1))
-    e_al, e_vx = xpair(0, al), [xcopy(2, vx, 0, CX, x_dn, padded=False)]
-    ez_al, ez_vz = zpair(0), [zcopy(2, z_dn)]
-    start(e_al + e_vx + ez_al + ez_vz)
+    e_al, ez_al = xpair(0), zpair(0)
+    start(e_al + ez_al)
+    loaded("vx")
+    loaded("vz")
+    xb[2] = vx[0].astype(BF16)
+    pack_z([(2, vz, 0, 0)])
+    e_vx, ez_vz = [xcopy(2, x_dn)], [zcopy(2, z_dn)]
+    start(e_vx + ez_vz)
 
     def a1_start(k, c):
         a, dev = a_peer(k)
@@ -189,11 +199,10 @@
 
     lax.fori_loop(1, GA, a1_start, 0)
     r1[a_me] = s1[a_me]
-
-    for c in loads["p0"]:
-        c.wait()
+    loaded("p0")
+    pack_x(3, p0)
     pack_z([(3, p0, 1, ROW0 + CZ - 1), (4, p0, 1, ROW0)])
-    e_p0, ez_p0 = xpair(3, p0), zpair(3)
+    e_p0, ez_p0 = xpair(3), zpair(3)
     start(e_p0 + ez_p0)
 
     place_t = jnp.broadcast_to(place.astype(F32), (LANES, PAN)).T
@@ -259,7 +268,7 @@
             rr[x, :, pl.ds(z * 8, 8), :] = 0.5 * inv
             d, cm = right, cp
 
-    def sweep(p, store, xs, z):
+    def sweep(p, store, source, xs, z):
         left, mid = at(p, xs[0], z), at(p, xs[0] + 1, z)
         for x in xs:
             right = at(p, x + 2, z)
@@ -267,9 +276,17 @@
                 x, z,
                 (raw(axm, x, z) * left + raw(axp, x, z) * right)
                 + (raw(azm, x, z) * at(p, x + 1, z, -1) + raw(azp, x, z) * at(p, x + 1, z, 1))
-                + (raw(aym, x, z) * y_minus(mid) + raw(ayp, x, z) * y_plus(mid) - raw(rr, x, z)),
+                + (raw(aym, x, z) * y_minus(mid) + raw(ayp, x, z) * y_plus(mid) - source(x, z)),
             )
             left, mid = mid, right
+
+    def scaled(x, z):
+        r = raw(rr, x, z) * raw(div, x, z)
+        rr[x, :, pl.ds(z * 8, 8), :] = r
+        return r
+
+    def kept(x, z):
+        return raw(rr, x, z)
 
     def into(ref):
         def store(x, z, v):
@@ -278,13 +295,13 @@
         return store
 
     def sweep1(xs, z):
-        sweep(p0, into(p1), xs, z)
+        sweep(p0, into(p1), scaled, xs, z)
 
     def sweep2(xs, z):
-        sweep(p1, into(p2), xs, z)
+        sweep(p1, into(p2), kept, xs, z)
 
     def sweep3(xs, z):
-        sweep(p2, lambda x, z, v: to_out(press_o, x, z, v), xs, z)
+        sweep(p2, lambda x, z, v: to_out(press_o, x, z, v), kept, xs, z)
 
     tiles = CZ // 8
     middle = tuple(range(1, CX - 1))
@@ -342,40 +359,26 @@
         s2[b, 0:REC_B, :] = got[b * REC_B : (b + 1) * REC_B]
         s2[b, REC_B:, :] = m1
 
+    def b1_start(k, c):
+        b, dev = b_peer(k)
+        rcopy(s2.at[b], r2.at[b_me], b1s.at[k], b1r.at[k], dev).start()
+        return c
+
+    lax.fori_loop(1, GB, b1_start, 0)
+    r2[b_me] = s2[b_me]
+
     recv(e_al + e_vx)
-    zero_x(al)
-
-    @pl.when(slab == SLABS - 1)
-    def _():
-        vx[CX] = jnp.zeros((NB, CZ, LANES), F32)
-
+    fill_x(0, al)
+    vx[CX] = jnp.where(slab == SLABS - 1, 0.0, xr[2].astype(F32))
     ends(advect)
-    e_rho, ez_rho = xpair(5, rho), zpair(5)
+    pack_x(5, rho)
+    e_rho, ez_rho = xpair(5), zpair(5)
     start(e_rho)
     pack_z([(5, rho, 1, ROW0 + CZ - 1), (6, rho, 1, ROW0)])
     start(ez_rho)
 
-    def b1_start(k, c):
-        b, dev = b_peer(k)
-        rcopy(s2.at[b], r2.at[b_me], b1s.at[k], b1r.at[k], dev).start()
-        return c
-
-    lax.fori_loop(1, GB, b1_start, 0)
-    r2[b_me] = s2[b_me]
-
     interior(coefficients, 1, inside)
-    recv(ez_p0 + ez_rho)
-    fill_z([
-        (3, p0, 1, ROW0 - 1, 0), (4, p0, 1, ROW0 + CZ, DEPTHS - 1),
-        (5, rho, 1, ROW0 - 1, 0), (6, rho, 1, ROW0 + CZ, DEPTHS - 1),
-    ])
-    edges(coefficients)
-    recv(e_p0 + e_rho)
-    zero_x(p0)
-    zero_x(rho)
-    ends(coefficients)
-    for c in loads["div"]:
-        c.wait()
+    loaded("div")
 
     def b1_wait(k, c):
         src = (b_me + GB - k) % GB
@@ -407,13 +410,24 @@
             x = i * 4 + k
             for y in range(NB):
                 part = h[k * CZ : (k + 1) * CZ, y * LANES : (y + 1) * LANES]
-                rr[x, y] = (div[x, y] + part) * rr[x, y]
+                div[x, y] += part
         return c
 
     lax.fori_loop(0, CX // 4, hull, 0)
 
+    recv(ez_p0 + ez_rho)
+    fill_z([
+        (3, p0, 1, ROW0 - 1, 0), (4, p0, 1, ROW0 + CZ, DEPTHS - 1),
+        (5, rho, 1, ROW0 - 1, 0), (6, rho, 1, ROW0 + CZ, DEPTHS - 1),
+    ])
+    edges(coefficients)
+    recv(e_p0 + e_rho)
+    fill_x(3, p0)
+    fill_x(5, rho)
+    ends(coefficients)
     ends(sweep1)
-    e_p1, ez_p1 = xpair(7, p1), zpair(7)
+    pack_x(7, p1)
+    e_p1, ez_p1 = xpair(7), zpair(7)
     start(e_p1)
     edges(sweep1)
     pack_z([(7, p1, 1, ROW0 + CZ - 1), (8, p1, 1, ROW0)])
@@ -427,9 +441,10 @@
     recv(ez_p1)
     fill_z([(7, p1, 1, ROW0 - 1, 0), (8, p1, 1, ROW0 + CZ, DEPTHS - 1)])
     recv(e_p1)
-    zero_x(p1)
+    fill_x(7, p1)
     ends(sweep2)
-    e_p2, ez_p2 = xpair(9, p2), zpair(9)
+    pack_x(9, p2)
+    e_p2, ez_p2 = xpair(9), zpair(9)
     start(e_p2)
     edges(sweep2)
     pack_z([(9, p2, 1, ROW0 + CZ - 1), (10, p2, 1, ROW0)])
@@ -439,13 +454,19 @@
     recv(ez_p2)
     fill_z([(9, p2, 1, ROW0 - 1, 0), (10, p2, 1, ROW0 + CZ, DEPTHS - 1)])
     edges(sweep3)
+    for x in range(2, CX - 2):
+        pb[x * CZ : (x + 1) * CZ, :] = press_o[x].astype(BF16)
+    acc[...] = dot(g_s[:, 2 * CZ : (CX - 2) * CZ], pb[2 * CZ : (CX - 2) * CZ, :])
     recv(e_p2)
-    zero_x(p2)
+    fill_x(9, p2)
     ends(sweep3)
 
-    for x in range(CX):
+    for x in (0, 1, CX - 2, CX - 1):
         pb[x * CZ : (x + 1) * CZ, :] = press_o[x].astype(BF16)
-    wet = dot(g_s[...], pb[...])
+    wet = acc[...] + (
+        dot(g_s[:, 0 : 2 * CZ], pb[0 : 2 * CZ, :])
+        + dot(g_s[:, (CX - 2) * CZ :], pb[(CX - 2) * CZ :, :])
+    )
     back = jnp.zeros((SLOTS, LANES), F32)
     for y in range(NB):
         back = jnp.where(block_c == y, wet[:, y * LANES : (y + 1) * LANES], back)
@@ -504,19 +525,29 @@
     lax.fori_loop(1, GA, a_done, 0)
 
 
+def deliver(press, alpha, panel, press_o, alpha_o, panel_o, sem):
+    pairs = ((press, press_o), (alpha, alpha_o), (panel, panel_o))
+    copies = [pltpu.make_async_copy(s, d, sem.at[i]) for i, (s, d) in enumerate(pairs)]
+    for c in copies:
+        c.start()
+    for c in copies:
+        c.wait()
+
+
 def body(alpha, vel_x, vel_z, divergence, press_guess, panel_records, panel_dest, panel_segment):
     padded = pltpu.VMEM((CX + 2, NB, PADZ, LANES), F32)
     plain = pltpu.VMEM((CX, NB, CZ, LANES), F32)
-    hbm = pl.BlockSpec(memory_space=pl.ANY)
+    hbm = pl.BlockSpec(memory_space=pltpu.HBM)
     vmem = pl.BlockSpec(memory_space=pltpu.VMEM)
     dma = lambda n: pltpu.SemaphoreType.DMA((n,))
     field = pltpu.VMEM((CX, CZ, BEAM), F32)
-    return pl.pallas_call(
+    outs = pl.pallas_call(
         kernel,
         out_shape=(field, field, pltpu.VMEM((PAN, LANES), BF16)),
-        in_specs=[hbm] * 5 + [vmem] * 3,
+        in_specs=[hbm] * 8,
         out_specs=(vmem, vmem, vmem),
         scratch_shapes=[
+            pltpu.VMEM((PAN, LANES), BF16), pltpu.VMEM((1, PAN), I32), pltpu.VMEM((1, PAN), I32),
             padded,
             pltpu.VMEM((CX + 1, NB, CZ, LANES), F32),
             pltpu.VMEM((CX, NB, CZ + 8, LANES), F32),
@@ -525,6 +556,9 @@
             plain, plain, plain, plain, plain, plain, plain,
             pltpu.VMEM((11, CX, NB, LANES), F32),
             pltpu.VMEM((11, CX, NB, LANES), F32),
+            pltpu.VMEM((11, NB, CZ, LANES), BF16),
+            pltpu.VMEM((11, NB, CZ, LANES), BF16),
+            pltpu.VMEM((SLOTS, BEAM), F32),
             pltpu.VMEM((GA, REC_A + META, LANES), BF16),
             pltpu.VMEM((GA, REC_A + META, LANES), BF16),
             pltpu.VMEM((GB, REC_B + META, LANES), BF16),
@@ -538,16 +572,25 @@
             pltpu.VMEM((SLOTS, SLOTS), BF16),
             pltpu.VMEM((SLOTS, BEAM), BF16),
             pltpu.VMEM((CX * CZ, BEAM), BF16),
-            dma(20), dma(11), dma(11), dma(11), dma(11),
+            dma(23), dma(11), dma(11), dma(11), dma(11),
             dma(GB), dma(GB), dma(GA), dma(GA), dma(GA), dma(GA), dma(GB), dma(GB),
         ],
         compiler_params=pltpu.CompilerParams(
-            collective_id=0, has_side_effects=True, vmem_limit_bytes=59 * 1024 * 1024 + 768 * 1024
+            collective_id=0, has_side_effects=True, vmem_limit_bytes=50 * 1024 * 1024
         ),
     )(
         alpha, vel_x, vel_z, divergence, press_guess, panel_records,
         panel_dest.reshape(1, PAN), panel_segment.reshape(1, PAN),
     )
+    outs = [pltpu.with_memory_space_constraint(o, pltpu.VMEM) for o in outs]
+    return pl.pallas_call(
+        deliver,
+        out_shape=tuple(jax.ShapeDtypeStruct(o.shape, o.dtype) for o in outs),
+        in_specs=[pl.BlockSpec(memory_space=pl.ANY)] * 3,
+        out_specs=(hbm,) * 3,
+        scratch_shapes=[dma(3)],
+        compiler_params=pltpu.CompilerParams(vmem_limit_bytes=1024 * 1024),
+    )(*outs)
 
 
 def solution(mesh):

time: 50.5 us -> 48.1 us (0.952)
  local copies, waits for them, and re-layouts: 3.27 us -> 0 us
  Pallas kernels: 46.5 us -> 47.3 us
    unnamed x3 -> x0, local copies, waits for them, and re-layouts: 3.27 us -> none
    pallas_call x0 -> x1, Pallas kernels: none -> 2.04 us  [body(): pl.pallas_call(deliver, out_shape=tuple((jax.ShapeDtypeStruct(o.shape, o....]
    pallas_call x1, Pallas kernels: 46.5 us -> 45.3 us  [body(): pl.pallas_call(kernel, out_shape=(field, field, pltpu.VMEM((PAN, LANES),...]
where the time goes in v3:
time: 48.1 us; the launch traced here: 47.9 us
  Pallas kernels  47.3 us (98%)
  between operations  0.64 us (1%)
    pallas_call x1, Pallas kernels, body(): pl.pallas_call(kernel, out_shape=(field, field, pltpu.VMEM((PAN, LANES),...  45.3 us
    pallas_call x1, Pallas kernels, body(): pl.pallas_call(deliver, out_shape=tuple((jax.ShapeDtypeStruct(o.shape, o....  2.04 us

profile of v3, /device:TPU:1, one launch (start us, length us, event | category | flops | bytes accessed | tf_op | source)
XLA Modules:
  0.0 47.9 jit_solution(8083537422961510924)
XLA Ops:
  0.6 45.3 %shard_map.103 = (f32[16,64,512]{2,1,0:T(8,128)S(1)}, f32[16,64,512]{2,1,0:T(8,128)S(1)}, bf16[256,128]{1,0:T(8,128)(2,1)S(1)}) custom-call(f32[16,64,512]{2,1,0:T(8,128)} %alpha_h.1, f32[16,64,512]{2,1,0:T(8,128)} %velx_h.1, f32[16,64,512]{2,1,0:T(8,128)} %velz_h.1, f32[16,64,512]{2,1,0:T(8,128)} %div_h.1, f32[16,64,512]{2,1,0:T(8,128)} %press_h.1, ...), custom_call_target="tpu_custom_call" | custom-call | tf_op jit(solution)/shard_map/pallas_call | solution.py:544
  45.9 2.0 %shard_map.104 = (f32[16,64,512]{2,1,0:T(8,128)}, f32[16,64,512]{2,1,0:T(8,128)}, bf16[256,128]{1,0:T(8,128)(2,1)}) custom-call(f32[16,64,512]{2,1,0:T(8,128)S(1)} %get-tuple-element.6.press, f32[16,64,512]{2,1,0:T(8,128)S(1)} %get-tuple-element.7.alpha, bf16[256,128]{1,0:T(8,128)(2,1)S(1)} %get-tuple-element.8.panel), custom_call_target="tpu_custom_call" | custom-call | tf_op jit(solution)/shard_map/pallas_call | solution.py:586

commit v4 on v3

--- a/solution.py
+++ b/solution.py
@@ -43,10 +43,10 @@
     rec_ref, dest_ref, seg_ref, al, vx, vz, div, rho, p0, p1, p2,
     axm, axp, azm, azp, aym, ayp, rr,
     zs, zr, xb, xr, acc,
-    s1, r1, s2, r2, s3, t1, s4, t2,
+    s1, r1, s2, r2, wb, tb,
     q_s, g_s, perm_s, rmat, pb,
     load_sem, xs_sem, xr_sem, zs_sem, zr_sem,
-    b1s, b1r, a1s, a1r, a2s, a2r, b2s, b2r,
+    b1s, b1r, a1s, a1r, home_s, home_r,
 ):
     slab = lax.axis_index("slab")
     depth = lax.axis_index("depth")
@@ -56,6 +56,7 @@
     z_up, z_dn = (slab, up_d), (slab, dn_d)
     b_me, core = slab // 2, slab % 2
     a_me = core * DEPTHS + depth
+    me = slab * DEPTHS + depth
 
     def b_peer(k):
         b = (b_me + k) % GB
@@ -179,10 +180,19 @@
             c.start()
         sends.extend(copies)
 
+    pl.semaphore_wait(barrier, 4 + (GB - 1) + (GA - 1))
+
+    def a1_start(k, c):
+        a, dev = a_peer(k)
+        rcopy(s1.at[a], r1.at[a_me], a1s.at[k], a1r.at[k], dev).start()
+        return c
+
+    lax.fori_loop(1, GA, a1_start, 0)
+    r1[a_me] = s1[a_me]
+
     loaded("al")
     pack_x(0, al)
     pack_z([(0, al, 1, ROW0 + CZ - 1), (1, al, 1, ROW0)])
-    pl.semaphore_wait(barrier, 4 + (GB - 1) + (GA - 1))
     e_al, ez_al = xpair(0), zpair(0)
     start(e_al + ez_al)
     loaded("vx")
@@ -192,20 +202,14 @@
     e_vx, ez_vz = [xcopy(2, x_dn)], [zcopy(2, z_dn)]
     start(e_vx + ez_vz)
 
-    def a1_start(k, c):
-        a, dev = a_peer(k)
-        rcopy(s1.at[a], r1.at[a_me], a1s.at[k], a1r.at[k], dev).start()
-        return c
-
-    lax.fori_loop(1, GA, a1_start, 0)
-    r1[a_me] = s1[a_me]
     loaded("p0")
     pack_x(3, p0)
     pack_z([(3, p0, 1, ROW0 + CZ - 1), (4, p0, 1, ROW0)])
     e_p0, ez_p0 = xpair(3), zpair(3)
     start(e_p0 + ez_p0)
 
-    place_t = jnp.broadcast_to(place.astype(F32), (LANES, PAN)).T
+    answer = dest * CAP + slot.astype(I32)
+    place_t = jnp.broadcast_to(answer.astype(F32), (LANES, PAN)).T
     for c in range(SLOTS // LANES):
         q_s[:, c * LANES : (c + 1) * LANES] = onehot(
             place_t == (iota((PAN, LANES), 1) + c * LANES).astype(F32)
@@ -336,10 +340,6 @@
             c.wait_recv()
 
     interior(advect, 1, inside)
-    recv(ez_al + ez_vz)
-    fill_z([(0, al, 1, ROW0 - 1, 0), (1, al, 1, ROW0 + CZ, DEPTHS - 1), (2, vz, 0, CZ, DEPTHS - 1)])
-    edges(advect)
-
     def a1_wait(k, c):
         src = (a_me + GA - k) % GA
         rcopy(s1.at[src], r1.at[src], a1s.at[k], a1r.at[k], a_peer(k)[1]).wait_recv()
@@ -347,9 +347,6 @@
 
     lax.fori_loop(1, GA, a1_wait, 0)
     got = dot(perm_s[...], r1[:, 0:REC_A, :].reshape(SLOTS, LANES)).astype(BF16)
-    perm_s[...] = onehot(
-        pc == (((pr >> 2) & (GB - 1)) * REC_B + (pr >> 6) * CAP + (pr & 3))
-    )
     mrow = iota((META, LANES), 0)
     m1 = jnp.zeros((META, LANES), F32)
     for a in range(GA):
@@ -366,6 +363,10 @@
 
     lax.fori_loop(1, GB, b1_start, 0)
     r2[b_me] = s2[b_me]
+
+    recv(ez_al + ez_vz)
+    fill_z([(0, al, 1, ROW0 - 1, 0), (1, al, 1, ROW0 + CZ, DEPTHS - 1), (2, vz, 0, CZ, DEPTHS - 1)])
+    edges(advect)
 
     recv(e_al + e_vx)
     fill_x(0, al)
@@ -403,18 +404,15 @@
             block_c == y, recs.astype(F32), 0.0
         ).astype(BF16)
 
-    def hull(i, c):
-        cells = (iota((4 * CZ, SLOTS), 0) + i * (4 * CZ)).astype(F32)
+    def hull(planes):
+        z = iota((CZ, SLOTS), 0)
+        cells = jnp.concatenate([z + x * CZ for x in planes], axis=0).astype(F32)
         h = dot(onehot(cells == key_r), rmat[...])
-        for k in range(4):
-            x = i * 4 + k
+        for k, x in enumerate(planes):
             for y in range(NB):
-                part = h[k * CZ : (k + 1) * CZ, y * LANES : (y + 1) * LANES]
-                div[x, y] += part
-        return c
-
-    lax.fori_loop(0, CX // 4, hull, 0)
-
+                div[x, y] += h[k * CZ : (k + 1) * CZ, y * LANES : (y + 1) * LANES]
+
+    hull((0, CX - 1))
     recv(ez_p0 + ez_rho)
     fill_z([
         (3, p0, 1, ROW0 - 1, 0), (4, p0, 1, ROW0 + CZ, DEPTHS - 1),
@@ -429,6 +427,8 @@
     pack_x(7, p1)
     e_p1, ez_p1 = xpair(7), zpair(7)
     start(e_p1)
+    for i in range(1, CX - 1, 7):
+        hull(tuple(range(i, i + 7)))
     edges(sweep1)
     pack_z([(7, p1, 1, ROW0 + CZ - 1), (8, p1, 1, ROW0)])
     start(ez_p1)
@@ -470,41 +470,20 @@
     back = jnp.zeros((SLOTS, LANES), F32)
     for y in range(NB):
         back = jnp.where(block_c == y, wet[:, y * LANES : (y + 1) * LANES], back)
-    back = back.astype(BF16)
-    for b in range(GB):
-        s3[b] = back[b * REC_B : (b + 1) * REC_B]
-
-    def b2_start(k, c):
-        b, dev = b_peer(k)
-        rcopy(s3.at[b], t1.at[b_me], b2s.at[k], b2r.at[k], dev).start()
-        return c
-
-    def b2_wait(k, c):
-        src = (b_me + GB - k) % GB
-        rcopy(s3.at[src], t1.at[src], b2s.at[k], b2r.at[k], b_peer(k)[1]).wait_recv()
-        return c
-
-    lax.fori_loop(1, GB, b2_start, 0)
-    t1[b_me] = s3[b_me]
-    lax.fori_loop(1, GB, b2_wait, 0)
-    turned = dot(perm_s[...], t1[...].reshape(SLOTS, LANES)).astype(BF16)
-    for a in range(GA):
-        s4[a] = turned[a * REC_A : (a + 1) * REC_A]
-
-    def a2_start(k, c):
-        a, dev = a_peer(k)
-        rcopy(s4.at[a], t2.at[a_me], a2s.at[k], a2r.at[k], dev).start()
-        return c
-
-    def a2_wait(k, c):
-        src = (a_me + GA - k) % GA
-        rcopy(s4.at[src], t2.at[src], a2s.at[k], a2r.at[k], a_peer(k)[1]).wait_recv()
-        return c
-
-    lax.fori_loop(1, GA, a2_start, 0)
-    t2[a_me] = s4[a_me]
-    lax.fori_loop(1, GA, a2_wait, 0)
-    panel_o[...] = dot(q_s[...], t2[...].reshape(SLOTS, LANES)).astype(BF16)
+    back = back.astype(BF16).astype(F32)
+    wb[...] = back.reshape(GA * GB, CAP, LANES)
+
+    def home(k, c):
+        d = (me + k) % (GA * GB)
+        rcopy(wb.at[d], tb.at[me], home_s, home_r, (d // DEPTHS, d % DEPTHS)).start()
+        return c
+
+    lax.fori_loop(1, GA * GB, home, 0)
+    others = pl.ds(0, GA * GB - 1)
+    tb[me] = wb[me]
+    pltpu.make_async_copy(wb.at[others], tb.at[others], home_r).wait()
+    panel_o[...] = dot(q_s[...], tb[...].reshape(SLOTS, LANES).astype(BF16)).astype(BF16)
+    pltpu.make_async_copy(wb.at[others], tb.at[others], home_s).wait()
 
     for c in sends:
         c.wait_send()
@@ -512,13 +491,11 @@
     def b_done(k, c):
         b, dev = b_peer(k)
         rcopy(s2.at[b], r2.at[b_me], b1s.at[k], b1r.at[k], dev).wait_send()
-        rcopy(s3.at[b], t1.at[b_me], b2s.at[k], b2r.at[k], dev).wait_send()
         return c
 
     def a_done(k, c):
         a, dev = a_peer(k)
         rcopy(s1.at[a], r1.at[a_me], a1s.at[k], a1r.at[k], dev).wait_send()
-        rcopy(s4.at[a], t2.at[a_me], a2s.at[k], a2r.at[k], dev).wait_send()
         return c
 
     lax.fori_loop(1, GB, b_done, 0)
@@ -563,17 +540,15 @@
             pltpu.VMEM((GA, REC_A + META, LANES), BF16),
             pltpu.VMEM((GB, REC_B + META, LANES), BF16),
             pltpu.VMEM((GB, REC_B + META, LANES), BF16),
-            pltpu.VMEM((GB, REC_B, LANES), BF16),
-            pltpu.VMEM((GB, REC_B, LANES), BF16),
-            pltpu.VMEM((GA, REC_A, LANES), BF16),
-            pltpu.VMEM((GA, REC_A, LANES), BF16),
+            pltpu.VMEM((GA * GB, CAP, LANES), F32),
+            pltpu.VMEM((GA * GB, CAP, LANES), F32),
             pltpu.VMEM((PAN, SLOTS), BF16),
             pltpu.VMEM((SLOTS, CX * CZ), BF16),
             pltpu.VMEM((SLOTS, SLOTS), BF16),
             pltpu.VMEM((SLOTS, BEAM), BF16),
             pltpu.VMEM((CX * CZ, BEAM), BF16),
             dma(23), dma(11), dma(11), dma(11), dma(11),
-            dma(GB), dma(GB), dma(GA), dma(GA), dma(GA), dma(GA), dma(GB), dma(GB),
+            dma(GB), dma(GB), dma(GA), dma(GA), pltpu.SemaphoreType.DMA, pltpu.SemaphoreType.DMA,
         ],
         compiler_params=pltpu.CompilerParams(
             collective_id=0, has_side_effects=True, vmem_limit_bytes=50 * 1024 * 1024

time: 48.1 us -> 45.1 us (0.938)
  Pallas kernels: 47.3 us -> 44.3 us
    pallas_call x1, Pallas kernels: 45.3 us -> 42.3 us  [body(): pl.pallas_call(kernel, out_shape=(field, field, pltpu.VMEM((PAN, LANES),...]
where the time goes in v4:
time: 45.1 us; the launch traced here: 45 us
  Pallas kernels  44.3 us (98%)
  between operations  0.64 us (1%)
    pallas_call x1, Pallas kernels, body(): pl.pallas_call(kernel, out_shape=(field, field, pltpu.VMEM((PAN, LANES),...  42.3 us
    pallas_call x1, Pallas kernels, body(): pl.pallas_call(deliver, out_shape=tuple((jax.ShapeDtypeStruct(o.shape, o....  2.04 us

profile of v4, /device:TPU:1, one launch (start us, length us, event | category | flops | bytes accessed | tf_op | source)
XLA Modules:
  0.0 45.0 jit_solution(8789209638097100197)
XLA Ops:
  0.6 42.3 %shard_map.103 = (f32[16,64,512]{2,1,0:T(8,128)S(1)}, f32[16,64,512]{2,1,0:T(8,128)S(1)}, bf16[256,128]{1,0:T(8,128)(2,1)S(1)}) custom-call(f32[16,64,512]{2,1,0:T(8,128)} %alpha_h.1, f32[16,64,512]{2,1,0:T(8,128)} %velx_h.1, f32[16,64,512]{2,1,0:T(8,128)} %velz_h.1, f32[16,64,512]{2,1,0:T(8,128)} %div_h.1, f32[16,64,512]{2,1,0:T(8,128)} %press_h.1, ...), custom_call_target="tpu_custom_call" | custom-call | tf_op jit(solution)/shard_map/pallas_call | solution.py:521
  42.9 2.0 %shard_map.104 = (f32[16,64,512]{2,1,0:T(8,128)}, f32[16,64,512]{2,1,0:T(8,128)}, bf16[256,128]{1,0:T(8,128)(2,1)}) custom-call(f32[16,64,512]{2,1,0:T(8,128)S(1)} %get-tuple-element.6.press, f32[16,64,512]{2,1,0:T(8,128)S(1)} %get-tuple-element.7.alpha, bf16[256,128]{1,0:T(8,128)(2,1)S(1)} %get-tuple-element.8.panel), custom_call_target="tpu_custom_call" | custom-call | tf_op jit(solution)/shard_map/pallas_call | solution.py:561

commit v5 on v4

--- a/solution.py
+++ b/solution.py
@@ -220,7 +220,6 @@
     )
 
     lane = iota((NB, 8, LANES), 2)
-    last = (lane == LANES - 1) & (iota((NB, 8, LANES), 0) == NB - 1)
     zero1 = jnp.zeros((1, 8, LANES), F32)
 
     def y_minus(v):
@@ -256,23 +255,34 @@
             rho[x + 1, :, pl.ds(ROW0 + z * 8, 8), :] = 1.0 + 9.0 * new
             a, fx0 = right, fx1
 
-    def coefficients(xs, z):
+    def first(xs, z):
         d = at(rho, xs[0] + 1, z)
         cm = recip(d + at(rho, xs[0], z))
+        left, mid = at(p0, xs[0], z), at(p0, xs[0] + 1, z)
         for x in xs:
-            right = at(rho, x + 2, z)
-            cp = recip(d + right)
+            beyond, right = at(rho, x + 2, z), at(p0, x + 2, z)
+            cp = recip(d + beyond)
             zm, zp = recip(d + at(rho, x + 1, z, -1)), recip(d + at(rho, x + 1, z, 1))
             ym = recip(d + y_minus(d))
             yp = y_plus(ym)
-            yp = jnp.where(last, recip(d), yp)
+            wall = jnp.where(lane[:1] == LANES - 1, recip(d[NB - 1 :]), yp[NB - 1 :])
+            yp = jnp.concatenate([yp[: NB - 1], wall], axis=0)
             inv = recip((cm + cp) + (zm + zp) + (ym + yp))
-            for ref, v in zip((axm, axp, azm, azp, aym, ayp), (cm, cp, zm, zp, ym, yp)):
-                ref[x, :, pl.ds(z * 8, 8), :] = v * inv
-            rr[x, :, pl.ds(z * 8, 8), :] = 0.5 * inv
-            d, cm = right, cp
-
-    def sweep(p, store, source, xs, z):
+            c = [v * inv for v in (cm, cp, zm, zp, ym, yp)]
+            for ref, v in zip((axm, axp, azm, azp, aym, ayp), c):
+                ref[x, :, pl.ds(z * 8, 8), :] = v
+            half = 0.5 * inv
+            r = raw(div, x, z) * half
+            rr[x, :, pl.ds(z * 8, 8), :] = r
+            div[x, :, pl.ds(z * 8, 8), :] = half
+            p1[x + 1, :, pl.ds(ROW0 + z * 8, 8), :] = (
+                (c[0] * left + c[1] * right)
+                + (c[2] * at(p0, x + 1, z, -1) + c[3] * at(p0, x + 1, z, 1))
+                + (c[4] * y_minus(mid) + c[5] * y_plus(mid) - r)
+            )
+            d, cm, left, mid = beyond, cp, mid, right
+
+    def sweep(p, store, xs, z):
         left, mid = at(p, xs[0], z), at(p, xs[0] + 1, z)
         for x in xs:
             right = at(p, x + 2, z)
@@ -280,17 +290,9 @@
                 x, z,
                 (raw(axm, x, z) * left + raw(axp, x, z) * right)
                 + (raw(azm, x, z) * at(p, x + 1, z, -1) + raw(azp, x, z) * at(p, x + 1, z, 1))
-                + (raw(aym, x, z) * y_minus(mid) + raw(ayp, x, z) * y_plus(mid) - source(x, z)),
+                + (raw(aym, x, z) * y_minus(mid) + raw(ayp, x, z) * y_plus(mid) - raw(rr, x, z)),
             )
             left, mid = mid, right
-
-    def scaled(x, z):
-        r = raw(rr, x, z) * raw(div, x, z)
-        rr[x, :, pl.ds(z * 8, 8), :] = r
-        return r
-
-    def kept(x, z):
-        return raw(rr, x, z)
 
     def into(ref):
         def store(x, z, v):
@@ -298,14 +300,11 @@
 
         return store
 
-    def sweep1(xs, z):
-        sweep(p0, into(p1), scaled, xs, z)
-
     def sweep2(xs, z):
-        sweep(p1, into(p2), kept, xs, z)
+        sweep(p1, into(p2), xs, z)
 
     def sweep3(xs, z):
-        sweep(p2, lambda x, z, v: to_out(press_o, x, z, v), kept, xs, z)
+        sweep(p2, lambda x, z, v: to_out(press_o, x, z, v), xs, z)
 
     tiles = CZ // 8
     middle = tuple(range(1, CX - 1))
@@ -333,7 +332,7 @@
 
         lax.fori_loop(0, tiles // 4, step, 0)
 
-    inside = tiles - 2
+    inside, early = tiles - 2, 5
 
     def recv(copies):
         for c in copies:
@@ -378,8 +377,14 @@
     pack_z([(5, rho, 1, ROW0 + CZ - 1), (6, rho, 1, ROW0)])
     start(ez_rho)
 
-    interior(coefficients, 1, inside)
     loaded("div")
+    interior(first, 1, inside)
+    recv(ez_p0 + ez_rho)
+    fill_z([
+        (3, p0, 1, ROW0 - 1, 0), (4, p0, 1, ROW0 + CZ, DEPTHS - 1),
+        (5, rho, 1, ROW0 - 1, 0), (6, rho, 1, ROW0 + CZ, DEPTHS - 1),
+    ])
+    edges(first)
 
     def b1_wait(k, c):
         src = (b_me + GB - k) % GB
@@ -392,12 +397,15 @@
     srow, scol = iota((SLOTS, GB * META), 0), iota((SLOTS, GB * META), 1)
     wide = dot(onehot(scol == (srow >> 5) * META + ((srow >> 2) & (GA - 1))), m2)
     pick = iota((SLOTS, LANES), 1) - (iota((SLOTS, LANES), 0) & 3) - b_me * CAP
-    hi_c = jnp.sum(jnp.where(pick == 0, wide, 0.0), axis=1, keepdims=True)
-    lo_c = jnp.sum(jnp.where(pick == REC_A, wide, 0.0), axis=1, keepdims=True)
-    seg_c = hi_c.astype(I32) * 64 + lo_c.astype(I32)
-    block_c, key_c = seg_c & 3, seg_c >> 2
-    key_f = jnp.broadcast_to(key_c, (SLOTS, LANES)).astype(F32)
-    key_r = key_f.T[0:1]
+    own_meta = jnp.where((pick == 0) | (pick == REC_A), wide, 0.0).astype(BF16)
+    weight_c = jnp.where(iota((LANES, LANES), 0) < REC_A, 64.0, 1.0).astype(BF16)
+    weight_r = jnp.where(iota((META, LANES), 1) < REC_A, 64.0, 1.0).astype(BF16)
+    seg_c = dot(own_meta, weight_c).astype(I32)
+    seg_r = lax.dot_general(
+        weight_r, own_meta, (((1,), (1,)), ((), ())), preferred_element_type=F32
+    )[0:1].astype(I32)
+    block_c, key_f = seg_c & 3, (seg_c >> 2).astype(F32)
+    key_r = (seg_r >> 2).astype(F32)
     recs = r2[:, 0:REC_B, :].reshape(SLOTS, LANES)
     for y in range(NB):
         rmat[:, y * LANES : (y + 1) * LANES] = jnp.where(
@@ -410,34 +418,27 @@
         h = dot(onehot(cells == key_r), rmat[...])
         for k, x in enumerate(planes):
             for y in range(NB):
-                div[x, y] += h[k * CZ : (k + 1) * CZ, y * LANES : (y + 1) * LANES]
-
-    hull((0, CX - 1))
-    recv(ez_p0 + ez_rho)
-    fill_z([
-        (3, p0, 1, ROW0 - 1, 0), (4, p0, 1, ROW0 + CZ, DEPTHS - 1),
-        (5, rho, 1, ROW0 - 1, 0), (6, rho, 1, ROW0 + CZ, DEPTHS - 1),
-    ])
-    edges(coefficients)
+                part = h[k * CZ : (k + 1) * CZ, y * LANES : (y + 1) * LANES] * div[x, y]
+                rr[x, y] += part
+                p1[x + 1, y, ROW0 : ROW0 + CZ, :] -= part
+
     recv(e_p0 + e_rho)
     fill_x(3, p0)
     fill_x(5, rho)
-    ends(coefficients)
-    ends(sweep1)
+    ends(first)
+    hull((0, CX - 1))
     pack_x(7, p1)
     e_p1, ez_p1 = xpair(7), zpair(7)
     start(e_p1)
     for i in range(1, CX - 1, 7):
         hull(tuple(range(i, i + 7)))
-    edges(sweep1)
     pack_z([(7, p1, 1, ROW0 + CZ - 1), (8, p1, 1, ROW0)])
     start(ez_p1)
-    interior(sweep1, 1, inside)
     for c in range(CX * CZ // LANES):
         g_s[:, c * LANES : (c + 1) * LANES] = onehot(
             key_f == (iota((SLOTS, LANES), 1) + c * LANES).astype(F32)
         )
-    interior(sweep2, 1, inside // 2)
+    interior(sweep2, 1, early)
     recv(ez_p1)
     fill_z([(7, p1, 1, ROW0 - 1, 0), (8, p1, 1, ROW0 + CZ, DEPTHS - 1)])
     recv(e_p1)
@@ -449,7 +450,7 @@
     edges(sweep2)
     pack_z([(9, p2, 1, ROW0 + CZ - 1), (10, p2, 1, ROW0)])
     start(ez_p2)
-    interior(sweep2, 1 + inside // 2, inside - inside // 2)
+    interior(sweep2, 1 + early, inside - early)
     interior(sweep3, 1, inside)
     recv(ez_p2)
     fill_z([(9, p2, 1, ROW0 - 1, 0), (10, p2, 1, ROW0 + CZ, DEPTHS - 1)])
@@ -473,12 +474,19 @@
     back = back.astype(BF16).astype(F32)
     wb[...] = back.reshape(GA * GB, CAP, LANES)
 
-    def home(k, c):
-        d = (me + k) % (GA * GB)
-        rcopy(wb.at[d], tb.at[me], home_s, home_r, (d // DEPTHS, d % DEPTHS)).start()
-        return c
-
-    lax.fori_loop(1, GA * GB, home, 0)
+    far = (2, 1, 3, 0)
+    for dz in far:
+        for dx in far:
+            b = (b_me // 4 + dz) % 4 * 4 + (b_me % 4 + dx) % 4
+
+            def home(k, c, b=b):
+                a = (a_me + k) % GA
+                d = b * GA + a
+                dev = (b * 2 + a // DEPTHS, a % DEPTHS)
+                rcopy(wb.at[d], tb.at[me], home_s, home_r, dev).start()
+                return c
+
+            lax.fori_loop(1 if dz == dx == 0 else 0, GA, home, 0)
     others = pl.ds(0, GA * GB - 1)
     tb[me] = wb[me]
     pltpu.make_async_copy(wb.at[others], tb.at[others], home_r).wait()

time: 45.1 us -> 45.2 us (level)
  no operation moved by 1% of the time
where the time goes in v5:
time: 45.2 us; the launch traced here: 45.1 us
  Pallas kernels  44.5 us (98%)
  between operations  0.64 us (1%)
    pallas_call x1, Pallas kernels, body(): pl.pallas_call(kernel, out_shape=(field, field, pltpu.VMEM((PAN, LANES),...  42.4 us
    pallas_call x1, Pallas kernels, body(): pl.pallas_call(deliver, out_shape=tuple((jax.ShapeDtypeStruct(o.shape, o....  2.04 us

profile of v5, /device:TPU:1, one launch (start us, length us, event | category | flops | bytes accessed | tf_op | source)
XLA Modules:
  0.0 45.1 jit_solution(4993576820990787411)
XLA Ops:
  0.6 42.4 %shard_map.103 = (f32[16,64,512]{2,1,0:T(8,128)S(1)}, f32[16,64,512]{2,1,0:T(8,128)S(1)}, bf16[256,128]{1,0:T(8,128)(2,1)S(1)}) custom-call(f32[16,64,512]{2,1,0:T(8,128)} %alpha_h.1, f32[16,64,512]{2,1,0:T(8,128)} %velx_h.1, f32[16,64,512]{2,1,0:T(8,128)} %velz_h.1, f32[16,64,512]{2,1,0:T(8,128)} %div_h.1, f32[16,64,512]{2,1,0:T(8,128)} %press_h.1, ...), custom_call_target="tpu_custom_call" | custom-call | tf_op jit(solution)/shard_map/pallas_call | solution.py:529
  43.1 2.0 %shard_map.104 = (f32[16,64,512]{2,1,0:T(8,128)}, f32[16,64,512]{2,1,0:T(8,128)}, bf16[256,128]{1,0:T(8,128)(2,1)}) custom-call(f32[16,64,512]{2,1,0:T(8,128)S(1)} %get-tuple-element.6.press, f32[16,64,512]{2,1,0:T(8,128)S(1)} %get-tuple-element.7.alpha, bf16[256,128]{1,0:T(8,128)(2,1)S(1)} %get-tuple-element.8.panel), custom_call_target="tpu_custom_call" | custom-call | tf_op jit(solution)/shard_map/pallas_call | solution.py:569

commit v6 on v5

--- a/solution.py
+++ b/solution.py
@@ -40,7 +40,7 @@
 def kernel(
     alpha_h, velx_h, velz_h, div_h, press_h, rec_h, dest_h, seg_h,
     press_o, alpha_o, panel_o,
-    rec_ref, dest_ref, seg_ref, al, vx, vz, div, rho, p0, p1, p2,
+    stage, rec_ref, dest_ref, seg_ref, al, vx, vz, div, rho, p0, p1, p2,
     axm, axp, azm, azp, aym, ayp, rr,
     zs, zr, xb, xr, acc,
     s1, r1, s2, r2, wb, tb,
@@ -85,10 +85,13 @@
     def field(src, dst):
         return [(src.at[:, :, pl.ds(y * LANES, LANES)], dst(y)) for y in range(NB)]
 
+    load("planes", [
+        (alpha_h.at[CX - 1], stage.at[0]), (alpha_h.at[0], stage.at[1]), (velx_h.at[0], stage.at[2]),
+    ])
     load("panels", [(dest_h, dest_ref), (seg_h, seg_ref), (rec_h, rec_ref)])
     load("al", field(alpha_h, lambda y: al.at[pl.ds(1, CX), y, pl.ds(ROW0, CZ), :]))
+    load("vz", field(velz_h, lambda y: vz.at[:, y, pl.ds(0, CZ), :]))
     load("vx", field(velx_h, lambda y: vx.at[pl.ds(0, CX), y, :, :]))
-    load("vz", field(velz_h, lambda y: vz.at[:, y, pl.ds(0, CZ), :]))
     load("p0", field(press_h, lambda y: p0.at[pl.ds(1, CX), y, pl.ds(ROW0, CZ), :]))
     load("div", field(div_h, lambda y: div.at[:, y, :, :]))
 
@@ -106,6 +109,68 @@
 
     lax.fori_loop(1, GB, sig_b, 0)
     lax.fori_loop(1, GA, sig_a, 0)
+
+    def rcopy(src, dst, ss, rs, dev):
+        return pltpu.make_async_remote_copy(
+            src_ref=src, dst_ref=dst, send_sem=ss, recv_sem=rs,
+            device_id=dev, device_id_type=MESH,
+        )
+
+    def xcopy(i, dev):
+        return rcopy(xb.at[i], xr.at[i], xs_sem.at[i], xr_sem.at[i], dev)
+
+    def zcopy(i, dev):
+        return rcopy(zs.at[i], zr.at[i], zs_sem.at[i], zr_sem.at[i], dev)
+
+    def xpair(i):
+        return [xcopy(i, x_up), xcopy(i + 1, x_dn)]
+
+    def pack_x(i, ref):
+        xb[i] = ref[CX, :, ROW0 : ROW0 + CZ, :].astype(BF16)
+        xb[i + 1] = ref[1, :, ROW0 : ROW0 + CZ, :].astype(BF16)
+
+    def fill_x(i, ref):
+        low, high = xr[i].astype(F32), xr[i + 1].astype(F32)
+        ref[0, :, ROW0 : ROW0 + CZ, :] = jnp.where(slab == 0, 0.0, low)
+        ref[CX + 1, :, ROW0 : ROW0 + CZ, :] = jnp.where(slab == SLABS - 1, 0.0, high)
+
+    def zpair(i):
+        return [zcopy(i, z_up), zcopy(i + 1, z_dn)]
+
+    def pack_z(items):
+        def step(g, c):
+            for k in range(4):
+                x = g * 4 + k
+                for i, ref, xo, r in items:
+                    zs[i, x] = ref[x + xo, :, r, :]
+            return c
+
+        lax.fori_loop(0, CX // 4, step, 0)
+
+    def fill_z(items):
+        def step(g, c):
+            for k in range(4):
+                x = g * 4 + k
+                for i, ref, xo, r, edge in items:
+                    ref[x + xo, :, r, :] = jnp.where(depth == edge, 0.0, zr[i, x])
+            return c
+
+        lax.fori_loop(0, CX // 4, step, 0)
+
+    sends = []
+
+    def start(copies):
+        for c in copies:
+            c.start()
+        sends.extend(copies)
+
+    loaded("planes")
+    for i in range(3):
+        for y in range(NB):
+            xb[i, y] = stage[i, :, y * LANES : (y + 1) * LANES].astype(BF16)
+    pl.semaphore_wait(barrier, 4 + (GB - 1) + (GA - 1))
+    e_al, e_vx = xpair(0), [xcopy(2, x_dn)]
+    start(e_al + e_vx)
 
     loaded("panels")
     dest, seg = dest_ref[...], seg_ref[...]
@@ -126,62 +191,6 @@
         s1[a, 0:REC_A, :] = packed[a * REC_A : (a + 1) * REC_A]
         s1[a, REC_A:, :] = jnp.broadcast_to(meta[a : a + 1], (META, LANES)).astype(BF16)
 
-    def rcopy(src, dst, ss, rs, dev):
-        return pltpu.make_async_remote_copy(
-            src_ref=src, dst_ref=dst, send_sem=ss, recv_sem=rs,
-            device_id=dev, device_id_type=MESH,
-        )
-
-    def xcopy(i, dev):
-        return rcopy(xb.at[i], xr.at[i], xs_sem.at[i], xr_sem.at[i], dev)
-
-    def zcopy(i, dev):
-        return rcopy(zs.at[i], zr.at[i], zs_sem.at[i], zr_sem.at[i], dev)
-
-    def xpair(i):
-        return [xcopy(i, x_up), xcopy(i + 1, x_dn)]
-
-    def pack_x(i, ref):
-        xb[i] = ref[CX, :, ROW0 : ROW0 + CZ, :].astype(BF16)
-        xb[i + 1] = ref[1, :, ROW0 : ROW0 + CZ, :].astype(BF16)
-
-    def fill_x(i, ref):
-        low, high = xr[i].astype(F32), xr[i + 1].astype(F32)
-        ref[0, :, ROW0 : ROW0 + CZ, :] = jnp.where(slab == 0, 0.0, low)
-        ref[CX + 1, :, ROW0 : ROW0 + CZ, :] = jnp.where(slab == SLABS - 1, 0.0, high)
-
-    def zpair(i):
-        return [zcopy(i, z_up), zcopy(i + 1, z_dn)]
-
-    def pack_z(items):
-        def step(g, c):
-            for k in range(4):
-                x = g * 4 + k
-                for i, ref, xo, r in items:
-                    zs[i, x] = ref[x + xo, :, r, :]
-            return c
-
-        lax.fori_loop(0, CX // 4, step, 0)
-
-    def fill_z(items):
-        def step(g, c):
-            for k in range(4):
-                x = g * 4 + k
-                for i, ref, xo, r, edge in items:
-                    ref[x + xo, :, r, :] = jnp.where(depth == edge, 0.0, zr[i, x])
-            return c
-
-        lax.fori_loop(0, CX // 4, step, 0)
-
-    sends = []
-
-    def start(copies):
-        for c in copies:
-            c.start()
-        sends.extend(copies)
-
-    pl.semaphore_wait(barrier, 4 + (GB - 1) + (GA - 1))
-
     def a1_start(k, c):
         a, dev = a_peer(k)
         rcopy(s1.at[a], r1.at[a_me], a1s.at[k], a1r.at[k], dev).start()
@@ -191,17 +200,11 @@
     r1[a_me] = s1[a_me]
 
     loaded("al")
-    pack_x(0, al)
-    pack_z([(0, al, 1, ROW0 + CZ - 1), (1, al, 1, ROW0)])
-    e_al, ez_al = xpair(0), zpair(0)
-    start(e_al + ez_al)
+    loaded("vz")
+    pack_z([(0, al, 1, ROW0 + CZ - 1), (1, al, 1, ROW0), (2, vz, 0, 0)])
+    ez_al, ez_vz = zpair(0), [zcopy(2, z_dn)]
+    start(ez_al + ez_vz)
     loaded("vx")
-    loaded("vz")
-    xb[2] = vx[0].astype(BF16)
-    pack_z([(2, vz, 0, 0)])
-    e_vx, ez_vz = [xcopy(2, x_dn)], [zcopy(2, z_dn)]
-    start(e_vx + ez_vz)
-
     loaded("p0")
     pack_x(3, p0)
     pack_z([(3, p0, 1, ROW0 + CZ - 1), (4, p0, 1, ROW0)])
@@ -434,10 +437,14 @@
         hull(tuple(range(i, i + 7)))
     pack_z([(7, p1, 1, ROW0 + CZ - 1), (8, p1, 1, ROW0)])
     start(ez_p1)
-    for c in range(CX * CZ // LANES):
+    tail = (CX - 2) * CZ
+    column = iota((SLOTS, LANES), 1)
+    for c in range(tail // LANES):
         g_s[:, c * LANES : (c + 1) * LANES] = onehot(
-            key_f == (iota((SLOTS, LANES), 1) + c * LANES).astype(F32)
+            key_f == (column + (c * LANES + CZ)).astype(F32)
         )
+    outer = jnp.where(column < CZ, column, column + tail)
+    g_s[:, tail:] = onehot(key_f == outer.astype(F32))
     interior(sweep2, 1, early)
     recv(ez_p1)
     fill_z([(7, p1, 1, ROW0 - 1, 0), (8, p1, 1, ROW0 + CZ, DEPTHS - 1)])
@@ -455,19 +462,16 @@
     recv(ez_p2)
     fill_z([(9, p2, 1, ROW0 - 1, 0), (10, p2, 1, ROW0 + CZ, DEPTHS - 1)])
     edges(sweep3)
-    for x in range(2, CX - 2):
-        pb[x * CZ : (x + 1) * CZ, :] = press_o[x].astype(BF16)
-    acc[...] = dot(g_s[:, 2 * CZ : (CX - 2) * CZ], pb[2 * CZ : (CX - 2) * CZ, :])
+    for x in range(1, CX - 1):
+        pb[(x - 1) * CZ : x * CZ, :] = press_o[x].astype(BF16)
+    acc[...] = dot(g_s[:, 0:tail], pb[0:tail, :])
     recv(e_p2)
     fill_x(9, p2)
     ends(sweep3)
 
-    for x in (0, 1, CX - 2, CX - 1):
-        pb[x * CZ : (x + 1) * CZ, :] = press_o[x].astype(BF16)
-    wet = acc[...] + (
-        dot(g_s[:, 0 : 2 * CZ], pb[0 : 2 * CZ, :])
-        + dot(g_s[:, (CX - 2) * CZ :], pb[(CX - 2) * CZ :, :])
-    )
+    pb[tail : tail + CZ, :] = press_o[0].astype(BF16)
+    pb[tail + CZ :, :] = press_o[CX - 1].astype(BF16)
+    wet = acc[...] + dot(g_s[:, tail:], pb[tail:, :])
     back = jnp.zeros((SLOTS, LANES), F32)
     for y in range(NB):
         back = jnp.where(block_c == y, wet[:, y * LANES : (y + 1) * LANES], back)
@@ -532,6 +536,7 @@
         in_specs=[hbm] * 8,
         out_specs=(vmem, vmem, vmem),
         scratch_shapes=[
+            pltpu.VMEM((3, CZ, BEAM), F32),
             pltpu.VMEM((PAN, LANES), BF16), pltpu.VMEM((1, PAN), I32), pltpu.VMEM((1, PAN), I32),
             padded,
             pltpu.VMEM((CX + 1, NB, CZ, LANES), F32),
@@ -555,7 +560,7 @@
             pltpu.VMEM((SLOTS, SLOTS), BF16),
             pltpu.VMEM((SLOTS, BEAM), BF16),
             pltpu.VMEM((CX * CZ, BEAM), BF16),
-            dma(23), dma(11), dma(11), dma(11), dma(11),
+            dma(26), dma(11), dma(11), dma(11), dma(11),
             dma(GB), dma(GB), dma(GA), dma(GA), pltpu.SemaphoreType.DMA, pltpu.SemaphoreType.DMA,
         ],
         compiler_params=pltpu.CompilerParams(

time: 45.2 us -> 45.6 us (level)
  no operation moved by 1% of the time
where the time goes in v6:
time: 45.6 us; the launch traced here: 45.5 us
  Pallas kernels  44.9 us (98%)
  between operations  0.64 us (1%)
    pallas_call x1, Pallas kernels, body(): pl.pallas_call(kernel, out_shape=(field, field, pltpu.VMEM((PAN, LANES),...  42.8 us
    pallas_call x1, Pallas kernels, body(): pl.pallas_call(deliver, out_shape=tuple((jax.ShapeDtypeStruct(o.shape, o....  2.04 us

profile of v6, /device:TPU:1, one launch (start us, length us, event | category | flops | bytes accessed | tf_op | source)
XLA Modules:
  0.0 45.5 jit_solution(7695748135177411928)
XLA Ops:
  0.6 42.8 %shard_map.103 = (f32[16,64,512]{2,1,0:T(8,128)S(1)}, f32[16,64,512]{2,1,0:T(8,128)S(1)}, bf16[256,128]{1,0:T(8,128)(2,1)S(1)}) custom-call(f32[16,64,512]{2,1,0:T(8,128)} %alpha_h.1, f32[16,64,512]{2,1,0:T(8,128)} %velx_h.1, f32[16,64,512]{2,1,0:T(8,128)} %velz_h.1, f32[16,64,512]{2,1,0:T(8,128)} %div_h.1, f32[16,64,512]{2,1,0:T(8,128)} %press_h.1, ...), custom_call_target="tpu_custom_call" | custom-call | tf_op jit(solution)/shard_map/pallas_call | solution.py:533
  43.5 2.0 %shard_map.104 = (f32[16,64,512]{2,1,0:T(8,128)}, f32[16,64,512]{2,1,0:T(8,128)}, bf16[256,128]{1,0:T(8,128)(2,1)}) custom-call(f32[16,64,512]{2,1,0:T(8,128)S(1)} %get-tuple-element.6.press, f32[16,64,512]{2,1,0:T(8,128)S(1)} %get-tuple-element.7.alpha, bf16[256,128]{1,0:T(8,128)(2,1)S(1)} %get-tuple-element.8.panel), custom_call_target="tpu_custom_call" | custom-call | tf_op jit(solution)/shard_map/pallas_call | solution.py:574

commit v7 on v6

--- a/solution.py
+++ b/solution.py
@@ -44,7 +44,7 @@
     axm, axp, azm, azp, aym, ayp, rr,
     zs, zr, xb, xr, acc,
     s1, r1, s2, r2, wb, tb,
-    q_s, g_s, perm_s, rmat, pb,
+    q_s, g_s, perm_s, spread, rmat, pb,
     load_sem, xs_sem, xr_sem, zs_sem, zr_sem,
     b1s, b1r, a1s, a1r, home_s, home_r,
 ):
@@ -85,10 +85,10 @@
     def field(src, dst):
         return [(src.at[:, :, pl.ds(y * LANES, LANES)], dst(y)) for y in range(NB)]
 
+    load("panels", [(dest_h, dest_ref), (seg_h, seg_ref), (rec_h, rec_ref)])
     load("planes", [
         (alpha_h.at[CX - 1], stage.at[0]), (alpha_h.at[0], stage.at[1]), (velx_h.at[0], stage.at[2]),
     ])
-    load("panels", [(dest_h, dest_ref), (seg_h, seg_ref), (rec_h, rec_ref)])
     load("al", field(alpha_h, lambda y: al.at[pl.ds(1, CX), y, pl.ds(ROW0, CZ), :]))
     load("vz", field(velz_h, lambda y: vz.at[:, y, pl.ds(0, CZ), :]))
     load("vx", field(velx_h, lambda y: vx.at[pl.ds(0, CX), y, :, :]))
@@ -163,14 +163,6 @@
         for c in copies:
             c.start()
         sends.extend(copies)
-
-    loaded("planes")
-    for i in range(3):
-        for y in range(NB):
-            xb[i, y] = stage[i, :, y * LANES : (y + 1) * LANES].astype(BF16)
-    pl.semaphore_wait(barrier, 4 + (GB - 1) + (GA - 1))
-    e_al, e_vx = xpair(0), [xcopy(2, x_dn)]
-    start(e_al + e_vx)
 
     loaded("panels")
     dest, seg = dest_ref[...], seg_ref[...]
@@ -191,12 +183,21 @@
         s1[a, 0:REC_A, :] = packed[a * REC_A : (a + 1) * REC_A]
         s1[a, REC_A:, :] = jnp.broadcast_to(meta[a : a + 1], (META, LANES)).astype(BF16)
 
+    pl.semaphore_wait(barrier, 4 + (GB - 1) + (GA - 1))
+
     def a1_start(k, c):
         a, dev = a_peer(k)
         rcopy(s1.at[a], r1.at[a_me], a1s.at[k], a1r.at[k], dev).start()
         return c
 
     lax.fori_loop(1, GA, a1_start, 0)
+    loaded("planes")
+    for i in range(3):
+        for y in range(NB):
+            xb[i, y] = stage[i, :, y * LANES : (y + 1) * LANES].astype(BF16)
+    e_al, e_vx = xpair(0), [xcopy(2, x_dn)]
+    start(e_al + e_vx)
+
     r1[a_me] = s1[a_me]
 
     loaded("al")
@@ -363,7 +364,8 @@
         rcopy(s2.at[b], r2.at[b_me], b1s.at[k], b1r.at[k], dev).start()
         return c
 
-    lax.fori_loop(1, GB, b1_start, 0)
+    for first_k, last_k in ((5, 12), (1, 5), (12, GB)):
+        lax.fori_loop(first_k, last_k, b1_start, 0)
     r2[b_me] = s2[b_me]
 
     recv(ez_al + ez_vz)
@@ -380,6 +382,8 @@
     pack_z([(5, rho, 1, ROW0 + CZ - 1), (6, rho, 1, ROW0)])
     start(ez_rho)
 
+    srow, scol = iota((SLOTS, GB * META), 0), iota((SLOTS, GB * META), 1)
+    spread[...] = onehot(scol == (srow >> 5) * META + ((srow >> 2) & (GA - 1)))
     loaded("div")
     interior(first, 1, inside)
     recv(ez_p0 + ez_rho)
@@ -388,6 +392,10 @@
         (5, rho, 1, ROW0 - 1, 0), (6, rho, 1, ROW0 + CZ, DEPTHS - 1),
     ])
     edges(first)
+    recv(e_p0 + e_rho)
+    fill_x(3, p0)
+    fill_x(5, rho)
+    ends(first)
 
     def b1_wait(k, c):
         src = (b_me + GB - k) % GB
@@ -397,8 +405,7 @@
     lax.fori_loop(1, GB, b1_wait, 0)
 
     m2 = r2[:, REC_B:, :].reshape(GB * META, LANES)
-    srow, scol = iota((SLOTS, GB * META), 0), iota((SLOTS, GB * META), 1)
-    wide = dot(onehot(scol == (srow >> 5) * META + ((srow >> 2) & (GA - 1))), m2)
+    wide = dot(spread[...], m2)
     pick = iota((SLOTS, LANES), 1) - (iota((SLOTS, LANES), 0) & 3) - b_me * CAP
     own_meta = jnp.where((pick == 0) | (pick == REC_A), wide, 0.0).astype(BF16)
     weight_c = jnp.where(iota((LANES, LANES), 0) < REC_A, 64.0, 1.0).astype(BF16)
@@ -425,10 +432,6 @@
                 rr[x, y] += part
                 p1[x + 1, y, ROW0 : ROW0 + CZ, :] -= part
 
-    recv(e_p0 + e_rho)
-    fill_x(3, p0)
-    fill_x(5, rho)
-    ends(first)
     hull((0, CX - 1))
     pack_x(7, p1)
     e_p1, ez_p1 = xpair(7), zpair(7)
@@ -558,6 +561,7 @@
             pltpu.VMEM((PAN, SLOTS), BF16),
             pltpu.VMEM((SLOTS, CX * CZ), BF16),
             pltpu.VMEM((SLOTS, SLOTS), BF16),
+            pltpu.VMEM((SLOTS, GB * META), BF16),
             pltpu.VMEM((SLOTS, BEAM), BF16),
             pltpu.VMEM((CX * CZ, BEAM), BF16),
             dma(26), dma(11), dma(11), dma(11), dma(11),

time: 45.6 us -> 45.2 us (level)
  Pallas kernels: 44.9 us -> 44.4 us
where the time goes in v7:
time: 45.2 us; the launch traced here: 45.1 us
  Pallas kernels  44.4 us (98%)
  between operations  0.64 us (1%)
    pallas_call x1, Pallas kernels, body(): pl.pallas_call(kernel, out_shape=(field, field, pltpu.VMEM((PAN, LANES),...  42.4 us
    pallas_call x1, Pallas kernels, body(): pl.pallas_call(deliver, out_shape=tuple((jax.ShapeDtypeStruct(o.shape, o....  2.04 us

profile of v7, /device:TPU:1, one launch (start us, length us, event | category | flops | bytes accessed | tf_op | source)
XLA Modules:
  0.0 45.1 jit_solution(9925622382889336345)
XLA Ops:
  0.6 42.4 %shard_map.103 = (f32[16,64,512]{2,1,0:T(8,128)S(1)}, f32[16,64,512]{2,1,0:T(8,128)S(1)}, bf16[256,128]{1,0:T(8,128)(2,1)S(1)}) custom-call(f32[16,64,512]{2,1,0:T(8,128)} %alpha_h.1, f32[16,64,512]{2,1,0:T(8,128)} %velx_h.1, f32[16,64,512]{2,1,0:T(8,128)} %velz_h.1, f32[16,64,512]{2,1,0:T(8,128)} %div_h.1, f32[16,64,512]{2,1,0:T(8,128)} %press_h.1, ...), custom_call_target="tpu_custom_call" | custom-call | tf_op jit(solution)/shard_map/pallas_call | solution.py:536
  43.0 2.0 %shard_map.104 = (f32[16,64,512]{2,1,0:T(8,128)}, f32[16,64,512]{2,1,0:T(8,128)}, bf16[256,128]{1,0:T(8,128)(2,1)}) custom-call(f32[16,64,512]{2,1,0:T(8,128)S(1)} %get-tuple-element.6.press, f32[16,64,512]{2,1,0:T(8,128)S(1)} %get-tuple-element.7.alpha, bf16[256,128]{1,0:T(8,128)(2,1)S(1)} %get-tuple-element.8.panel), custom_call_target="tpu_custom_call" | custom-call | tf_op jit(solution)/shard_map/pallas_call | solution.py:578

commit v8 on v7

--- a/solution.py
+++ b/solution.py
@@ -259,12 +259,12 @@
             rho[x + 1, :, pl.ds(ROW0 + z * 8, 8), :] = 1.0 + 9.0 * new
             a, fx0 = right, fx1
 
-    def first(xs, z):
+    def first(xs, z, also_sweep=True):
         d = at(rho, xs[0] + 1, z)
         cm = recip(d + at(rho, xs[0], z))
         left, mid = at(p0, xs[0], z), at(p0, xs[0] + 1, z)
         for x in xs:
-            beyond, right = at(rho, x + 2, z), at(p0, x + 2, z)
+            beyond, right = at(rho, x + 2, z), at(p0, x + 2, z) if also_sweep else None
             cp = recip(d + beyond)
             zm, zp = recip(d + at(rho, x + 1, z, -1)), recip(d + at(rho, x + 1, z, 1))
             ym = recip(d + y_minus(d))
@@ -279,12 +279,15 @@
             r = raw(div, x, z) * half
             rr[x, :, pl.ds(z * 8, 8), :] = r
             div[x, :, pl.ds(z * 8, 8), :] = half
+            d, cm, before, now = beyond, cp, left, mid
+            left, mid = mid, right
+            if not also_sweep:
+                continue
             p1[x + 1, :, pl.ds(ROW0 + z * 8, 8), :] = (
-                (c[0] * left + c[1] * right)
+                (c[0] * before + c[1] * right)
                 + (c[2] * at(p0, x + 1, z, -1) + c[3] * at(p0, x + 1, z, 1))
-                + (c[4] * y_minus(mid) + c[5] * y_plus(mid) - r)
+                + (c[4] * y_minus(now) + c[5] * y_plus(now) - r)
             )
-            d, cm, left, mid = beyond, cp, mid, right
 
     def sweep(p, store, xs, z):
         left, mid = at(p, xs[0], z), at(p, xs[0] + 1, z)
@@ -304,6 +307,12 @@
 
         return store
 
+    def coefficients(xs, z):
+        first(xs, z, also_sweep=False)
+
+    def sweep1(xs, z):
+        sweep(p0, into(p1), xs, z)
+
     def sweep2(xs, z):
         sweep(p1, into(p2), xs, z)
 
@@ -336,7 +345,7 @@
 
         lax.fori_loop(0, tiles // 4, step, 0)
 
-    inside, early = tiles - 2, 5
+    inside, early, fused = tiles - 2, 5, 2
 
     def recv(copies):
         for c in copies:
@@ -385,7 +394,8 @@
     srow, scol = iota((SLOTS, GB * META), 0), iota((SLOTS, GB * META), 1)
     spread[...] = onehot(scol == (srow >> 5) * META + ((srow >> 2) & (GA - 1)))
     loaded("div")
-    interior(first, 1, inside)
+    interior(first, 1, fused)
+    interior(coefficients, 1 + fused, inside - fused)
     recv(ez_p0 + ez_rho)
     fill_z([
         (3, p0, 1, ROW0 - 1, 0), (4, p0, 1, ROW0 + CZ, DEPTHS - 1),
@@ -440,6 +450,7 @@
         hull(tuple(range(i, i + 7)))
     pack_z([(7, p1, 1, ROW0 + CZ - 1), (8, p1, 1, ROW0)])
     start(ez_p1)
+    interior(sweep1, 1 + fused, inside - fused)
     tail = (CX - 2) * CZ
     column = iota((SLOTS, LANES), 1)
     for c in range(tail // LANES):

time: 45.2 us -> 43.6 us (0.965)
  Pallas kernels: 44.4 us -> 42.9 us
    pallas_call x1, Pallas kernels: 42.4 us -> 40.9 us  [body(): pl.pallas_call(kernel, out_shape=(field, field, pltpu.VMEM((PAN, LANES),...]
where the time goes in v8:
time: 43.6 us; the launch traced here: 43.5 us
  Pallas kernels  42.9 us (98%)
  between operations  0.64 us (1%)
    pallas_call x1, Pallas kernels, body(): pl.pallas_call(kernel, out_shape=(field, field, pltpu.VMEM((PAN, LANES),...  40.9 us
    pallas_call x1, Pallas kernels, body(): pl.pallas_call(deliver, out_shape=tuple((jax.ShapeDtypeStruct(o.shape, o....  2.04 us

profile of v8, /device:TPU:1, one launch (start us, length us, event | category | flops | bytes accessed | tf_op | source)
XLA Modules:
  0.0 43.5 jit_solution(1322095754309098109)
XLA Ops:
  0.6 40.9 %shard_map.103 = (f32[16,64,512]{2,1,0:T(8,128)S(1)}, f32[16,64,512]{2,1,0:T(8,128)S(1)}, bf16[256,128]{1,0:T(8,128)(2,1)S(1)}) custom-call(f32[16,64,512]{2,1,0:T(8,128)} %alpha_h.1, f32[16,64,512]{2,1,0:T(8,128)} %velx_h.1, f32[16,64,512]{2,1,0:T(8,128)} %velz_h.1, f32[16,64,512]{2,1,0:T(8,128)} %div_h.1, f32[16,64,512]{2,1,0:T(8,128)} %press_h.1, ...), custom_call_target="tpu_custom_call" | custom-call | tf_op jit(solution)/shard_map/pallas_call | solution.py:547
  41.5 2.0 %shard_map.104 = (f32[16,64,512]{2,1,0:T(8,128)}, f32[16,64,512]{2,1,0:T(8,128)}, bf16[256,128]{1,0:T(8,128)(2,1)}) custom-call(f32[16,64,512]{2,1,0:T(8,128)S(1)} %get-tuple-element.6.press, f32[16,64,512]{2,1,0:T(8,128)S(1)} %get-tuple-element.7.alpha, bf16[256,128]{1,0:T(8,128)(2,1)S(1)} %get-tuple-element.8.panel), custom_call_target="tpu_custom_call" | custom-call | tf_op jit(solution)/shard_map/pallas_call | solution.py:589

commit v9 on v8

--- a/solution.py
+++ b/solution.py
@@ -345,7 +345,7 @@
 
         lax.fori_loop(0, tiles // 4, step, 0)
 
-    inside, early, fused = tiles - 2, 5, 2
+    inside, early, fused = tiles - 2, 3, 0
 
     def recv(copies):
         for c in copies:

time: 43.6 us -> 43.2 us (level)
  Pallas kernels: 42.9 us -> 42.4 us
    pallas_call x1, Pallas kernels: 40.9 us -> 40.4 us  [body(): pl.pallas_call(kernel, out_shape=(field, field, pltpu.VMEM((PAN, LANES),...]
where the time goes in v9:
time: 43.2 us; the launch traced here: 43.1 us
  Pallas kernels  42.4 us (98%)
  between operations  0.64 us (1%)
    pallas_call x1, Pallas kernels, body(): pl.pallas_call(kernel, out_shape=(field, field, pltpu.VMEM((PAN, LANES),...  40.4 us
    pallas_call x1, Pallas kernels, body(): pl.pallas_call(deliver, out_shape=tuple((jax.ShapeDtypeStruct(o.shape, o....  2.04 us

profile of v9, /device:TPU:1, one launch (start us, length us, event | category | flops | bytes accessed | tf_op | source)
XLA Modules:
  0.0 43.1 jit_solution(5992254078563353548)
XLA Ops:
  0.6 40.4 %shard_map.103 = (f32[16,64,512]{2,1,0:T(8,128)S(1)}, f32[16,64,512]{2,1,0:T(8,128)S(1)}, bf16[256,128]{1,0:T(8,128)(2,1)S(1)}) custom-call(f32[16,64,512]{2,1,0:T(8,128)} %alpha_h.1, f32[16,64,512]{2,1,0:T(8,128)} %velx_h.1, f32[16,64,512]{2,1,0:T(8,128)} %velz_h.1, f32[16,64,512]{2,1,0:T(8,128)} %div_h.1, f32[16,64,512]{2,1,0:T(8,128)} %press_h.1, ...), custom_call_target="tpu_custom_call" | custom-call | tf_op jit(solution)/shard_map/pallas_call | solution.py:547
  41.0 2.0 %shard_map.104 = (f32[16,64,512]{2,1,0:T(8,128)}, f32[16,64,512]{2,1,0:T(8,128)}, bf16[256,128]{1,0:T(8,128)(2,1)}) custom-call(f32[16,64,512]{2,1,0:T(8,128)S(1)} %get-tuple-element.6.press, f32[16,64,512]{2,1,0:T(8,128)S(1)} %get-tuple-element.7.alpha, bf16[256,128]{1,0:T(8,128)(2,1)S(1)} %get-tuple-element.8.panel), custom_call_target="tpu_custom_call" | custom-call | tf_op jit(solution)/shard_map/pallas_call | solution.py:589
